TPU v7x, 32 devices: a whole 2x2x4 slice. The times are simulated.
32 devices in a mesh: dp: 4 (over x, core), pipe: 2 (over y), ctx: 4 (over z).
Axes of the slice: x: 2, y: 2, z: 4, core: 2. Of those that a mesh axis runs over, the one named last changes fastest.
Arguments:
- arriving: bfloat16 [2, 4, 512, 4096], P('pipe', 'dp', 'ctx'), may hold values from -6 to 6
- features: bfloat16 [2, 4, 512, 4096], P('pipe', 'dp', 'ctx'), may hold values from -6 to 6
- short_taps: float32 [2, 7, 4096], P('pipe'), may hold values from -2 to 2
- filters: float32 [2, 256, 512], P('pipe', 'ctx'), may hold values from -0.25 to 0.25
Outputs:
- feature_grads: bfloat16 [2, 4, 512, 4096], P('pipe', 'dp', 'ctx')
- filter_grads: float32 [2, 256, 512], P('pipe', 'ctx')
- tap_grads: float32 [2, 7, 4096], P('pipe', None, 'ctx')
All inputs are finite; a program needn't handle non-finite values.
Results may differ from a plain program's by a relative error of at most 0.0015.
Values may be sent and summed in bfloat16 or wider, within the bound.
A program may use at most 64 MiB of HBM per device.

v0:
```python
import math

import jax
import jax.numpy as jnp
from jax import lax
from jax.sharding import PartitionSpec as P

TABLE_PRECISION = lax.Precision.HIGH


def passed_along(value, axis, steps):
    count = lax.axis_size(axis)
    pairs = [(source, (source + steps) % count) for source in range(count)]
    return lax.ppermute(value, axis, pairs)


def phase_table(count_a, count_b, modulus):
    first_index = lax.broadcasted_iota(jnp.int32, (count_a, count_b), 0)
    second_index = lax.broadcasted_iota(jnp.int32, (count_a, count_b), 1)
    phase = (first_index * second_index % modulus).astype(jnp.float32) * (2.0 * math.pi / modulus)
    return (jnp.cos(phase), jnp.sin(phase))


def block_table(cos_part, sin_part):
    return jnp.stack(
        [
            jnp.concatenate([cos_part, -sin_part], axis=-1),
            jnp.concatenate([sin_part, cos_part], axis=-1),
        ]
    )


def split_length(seq_len):
    factor = 1
    for candidate in range(1, seq_len + 1):
        if seq_len % candidate == 0 and candidate * candidate <= 2 * seq_len:
            factor = candidate
    return factor


def finish_forward(first, inner_len, outer_len):
    full_len = inner_len * outer_len
    cos_turn, sin_turn = phase_table(inner_len, outer_len, full_len)
    first_re = first[..., :outer_len]
    first_im = first[..., outer_len:]
    turned = jnp.stack(
        [first_re * cos_turn + first_im * sin_turn, first_im * cos_turn - first_re * sin_turn],
        axis=-3,
    )
    cos_last, sin_last = phase_table(inner_len, inner_len, inner_len)
    return jnp.einsum(
        "...cnk,cne->...ke", turned, block_table(cos_last, sin_last), precision=TABLE_PRECISION
    )


def forward_pairs(values):
    inner_len = values.shape[-1]
    half_rows = values.shape[-2]
    outer_len = 2 * half_rows
    cos_first, sin_first = phase_table(half_rows, outer_len, outer_len)
    first = jnp.einsum(
        "fagmn,ame->fgne", values, block_table(cos_first, sin_first), precision=TABLE_PRECISION
    )
    return finish_forward(first, inner_len, outer_len)


def forward_real(values):
    inner_len = values.shape[-1]
    half_rows = values.shape[-2]
    outer_len = 2 * half_rows
    cos_first, sin_first = phase_table(half_rows, outer_len, outer_len)
    first = jnp.einsum(
        "fmn,me->fne", values, block_table(cos_first, sin_first)[0], precision=TABLE_PRECISION
    )
    return finish_forward(first, inner_len, outer_len)


def inverse_spectrum(spectrum, real_only):
    outer_len = spectrum.shape[-2]
    inner_len = spectrum.shape[-1] // 2
    half_rows = outer_len // 2
    full_len = outer_len * inner_len
    cos_first, sin_first = phase_table(inner_len, inner_len, inner_len)
    table_first = jnp.concatenate(
        [
            jnp.concatenate([cos_first, sin_first], axis=1),
            jnp.concatenate([-sin_first, cos_first], axis=1),
        ],
        axis=0,
    )
    step = jnp.einsum("...ke,ew->...kw", spectrum, table_first, precision=TABLE_PRECISION)
    step_re = step[..., :inner_len]
    step_im = step[..., inner_len:]
    cos_turn, sin_turn = phase_table(outer_len, inner_len, full_len)
    turned = jnp.stack(
        [step_re * cos_turn - step_im * sin_turn, step_re * sin_turn + step_im * cos_turn], axis=-3
    )
    cos_last, sin_last = phase_table(half_rows, outer_len, outer_len)
    table_last = jnp.stack(
        [jnp.stack([cos_last, -sin_last], axis=1), jnp.stack([sin_last, cos_last], axis=1)]
    )
    norm_factor = 1.0 / full_len
    if real_only:
        return (
            jnp.einsum("mck,...ckn->m...n", table_last[0], turned, precision=TABLE_PRECISION)
            * norm_factor
        )
    return (
        jnp.einsum("dmck,...ckn->dm...n", table_last, turned, precision=TABLE_PRECISION)
        * norm_factor
    )


def body(arriving, features, short_taps, filters):
    ctx_count = lax.axis_size("ctx")
    ctx_rank = lax.axis_index("ctx")
    dp_count = lax.axis_size("dp")
    rows_dev = features.shape[2]
    channels = features.shape[3]
    own_width = channels // ctx_count
    filter_count = filters.shape[1]
    group_size = own_width // filter_count
    half_group = group_size // 2
    taps_count = short_taps.shape[1]
    seq_len = filters.shape[2]
    inner_len = split_length(seq_len)
    half_rows = seq_len // inner_len
    feature_cols = features[0, 0].T
    arrived = passed_along(arriving, "pipe", -1)
    gradient_cols = arrived[0, 0].T
    gradient_block, feature_block = (
        lax.all_to_all(gradient_cols, "ctx", split_axis=0, concat_axis=1, tiled=True),
        lax.all_to_all(feature_cols, "ctx", split_axis=0, concat_axis=1, tiled=True),
    )
    tap_block = lax.dynamic_slice_in_dim(short_taps[0], ctx_rank * own_width, own_width, 1)
    feature_vals = feature_block.astype(jnp.float32)
    padded_feat = jnp.pad(feature_vals, ((0, 0), (taps_count - 1, 0)))
    conv_in = jnp.zeros(feature_vals.shape, jnp.float32)
    for offset in range(taps_count):
        conv_in = (
            conv_in
            + tap_block[offset][:, None]
            * padded_feat[:, taps_count - 1 - offset : taps_count - 1 - offset + seq_len]
        )
    pair_shape = (filter_count, 2, half_group, half_rows, inner_len)
    spectrum_u = forward_pairs(conv_in.reshape(pair_shape))
    spectrum_g = forward_pairs(gradient_block.astype(jnp.float32).reshape(pair_shape))
    spectrum_h = forward_real(filters[0].reshape(filter_count, half_rows, inner_len))[:, None]
    g_re = spectrum_g[..., :inner_len]
    g_im = spectrum_g[..., inner_len:]
    u_re = spectrum_u[..., :inner_len]
    u_im = spectrum_u[..., inner_len:]
    h_re = spectrum_h[..., :inner_len]
    h_im = spectrum_h[..., inner_len:]
    back = jnp.concatenate([h_re * g_re + h_im * g_im, h_re * g_im - h_im * g_re], axis=-1)
    lag = jnp.concatenate(
        [jnp.sum(g_re * u_re + g_im * u_im, axis=1), jnp.sum(g_im * u_re - g_re * u_im, axis=1)],
        axis=-1,
    )
    grad_blocks = inverse_spectrum(back, False)
    conv_in_grad = jnp.transpose(grad_blocks, (2, 0, 3, 1, 4)).reshape(own_width, seq_len)
    filter_part = jnp.transpose(inverse_spectrum(lag, True), (1, 0, 2)).reshape(
        filter_count, seq_len
    )
    padded_grad = jnp.pad(conv_in_grad, ((0, 0), (0, taps_count - 1)))
    feature_grad = jnp.zeros(conv_in_grad.shape, jnp.float32)
    tap_terms = []
    for offset in range(taps_count):
        feature_grad = (
            feature_grad + tap_block[offset][:, None] * padded_grad[:, offset : offset + seq_len]
        )
        tap_terms.append(
            jnp.sum(
                conv_in_grad
                * padded_feat[:, taps_count - 1 - offset : taps_count - 1 - offset + seq_len],
                axis=1,
            )
        )
    tap_part = jnp.stack(tap_terms)
    filter_total, tap_total = lax.psum((filter_part, tap_part), "dp")
    back_cols = feature_grad.astype(jnp.bfloat16)
    feature_rows = lax.all_to_all(back_cols, "ctx", split_axis=1, concat_axis=0, tiled=True)
    feature_grads = feature_rows.T.reshape(1, 1, rows_dev, channels)
    filter_scale = 1.0 / math.sqrt(dp_count * group_size * seq_len)
    tap_scale = 1.0 / math.sqrt(dp_count * seq_len)
    filter_grads = (filter_total * filter_scale)[None]
    tap_grads = (tap_total * tap_scale).reshape(1, taps_count, own_width)
    return (feature_grads, filter_grads, tap_grads)


def solution(mesh):
    in_specs = (
        P("pipe", "dp", "ctx", None),
        P("pipe", "dp", "ctx", None),
        P("pipe", None, None),
        P("pipe", "ctx", None),
    )
    out_specs = (P("pipe", "dp", "ctx", None), P("pipe", "ctx", None), P("pipe", None, "ctx"))
    return jax.shard_map(body, mesh=mesh, in_specs=in_specs, out_specs=out_specs, check_vma=False)
```

profile of v0, /device:TPU:0, one launch (start us, length us, event | category | flops | bytes accessed | tf_op | source)
XLA Modules:
  0.0 276.0 jit_solution(6566712052729913669)
XLA Ops:
  7.2 2.3 copy.77
  9.5 6.3 %all-to-all-start.2 = ((bf16[4,1024,128]{2,1,0:T(8,128)(2,1)}), bf16[4,1024,128]{2,1,0:T(8,128)(2,1)S(1)}, u32[]{:S(2)}, u32[]{:S(2)}) async-start(bf16[4,1024,128]{2,1,0:T(8,128)(2,1)} %bitcast.57), calls=%async_computation.2 | async-start | bytes 2097152 | tf_op jit(solution)/shard_map/all_to_all | solution.py:133
  20.0 20.7 %collective-permute-done = bf16[1,1,128,4096]{3,2,1,0:T(8,128)(2,1)} collective-permute-done((bf16[1,1,128,4096]{3,2,1,0:T(8,128)(2,1)}, bf16[1,1,128,4096]{3,2,1,0:T(8,128)(2,1)}, u32[]{:S(2)}, u32[]{:S(2)}) %collective-permute-start) | collective-permute-done | bytes 1048608 | tf_op jit(solution)/shard_map/ppermute | solution.py:14
  40.7 2.3 copy.67
  43.0 5.1 %all-to-all-start = ((bf16[4,1024,128]{2,1,0:T(8,128)(2,1)}), bf16[4,1024,128]{2,1,0:T(8,128)(2,1)}, u32[]{:S(2)}, u32[]{:S(2)}) async-start(bf16[4,1024,128]{2,1,0:T(8,128)(2,1)} %bitcast.23), calls=%async_computation | async-start | bytes 2097152 | tf_op jit(solution)/shard_map/all_to_all | solution.py:132
  52.4 2.7 copy.88
  57.1 5.6 %multiply_add_fusion.1 = f32[1024,512]{1,0:T(8,128)} fusion(f32[1024,512]{1,0:T(8,128)S(1)} %copy.79, f32[1024]{0:T(1024)S(1)} %bitcast.174, f32[1024]{0:T(1024)S(1)} %bitcast.164, f32[1024]{0:T(1024)S(1)} %bitcast.166, f32[1024]{0:T(1024)S(1)} %bitcast.168, f32[1024]{0:T(1024)S(1)} %bitcast.170, f32[1024]{0:T(1024)S(1)} %bitcast.172, f32[1024]{0:T(1024)S(1)} %bitcast.162), kind=kLoop, calls=%fused_computation.63 | loop fusion | flops 6815744 | bytes 4222976 | tf_op jit(solution)/shard_map/add | solution.py:141
  62.7 6.1 %reshape.181 = f32[64,2,8,16,32]{4,3,2,1,0:T(8,128)} reshape(f32[1024,512]{1,0:T(8,128)} %multiply_add_fusion.1) | data formatting | bytes 4194304 | tf_op jit(solution)/shard_map/reshape | solution.py:146
  68.8 8.8 %copy.81 = f32[64,2,8,16,32]{0,3,1,4,2:T(8,128)} copy(f32[64,2,8,16,32]{4,3,2,1,0:T(8,128)} %reshape.181) | data formatting | bytes 4194304 | tf_op jit(solution)/shard_map/reshape | solution.py:146
  77.6 6.3 %reshape.185 = f32[64,2,8,16,32]{4,3,2,1,0:T(8,128)} reshape(f32[1024,4,128]{2,1,0:T(4,128)} %copy.88) | data formatting | bytes 4194304 | tf_op jit(solution)/shard_map/convert_element_type | solution.py:136
  83.9 9.0 %copy.89 = f32[64,2,8,16,32]{0,3,4,2,1:T(8,128)} copy(f32[64,2,8,16,32]{4,3,2,1,0:T(8,128)} %reshape.185) | data formatting | bytes 4194304 | tf_op jit(solution)/shard_map/convert_element_type | solution.py:136
  93.0 8.9 %convolution_bitcast_fusion.1 = f32[64,8,32,64]{0,3,2,1:T(8,128)} fusion(f32[64,2,8,16,32]{0,3,1,4,2:T(8,128)} %copy.81, f32[1,16,64]{2,1,0:T(8,128)S(1)} %get-tuple-element.51, f32[1,16,64]{2,1,0:T(8,128)S(1)} %get-tuple-element.50), kind=kOutput, calls=%fused_computation.30 | convolution fusion | flops 201328640 | bytes 6299648 | tf_op jit(solution)/shard_map/fagmn,ame->fgne/dot_general | solution.py:61
  101.8 2.0 copy.68
  103.9 3.3 %reshape.178 = bf16[64,2,8,16,32]{4,3,2,1,0:T(8,128)(2,1)} reshape(bf16[1024,4,128]{2,1,0:T(4,128)(2,1)S(1)} %copy.68) | data formatting | bytes 2097152 | tf_op jit(solution)/shard_map/reshape | solution.py:147
  107.2 8.5 %copy.69 = bf16[64,2,8,16,32]{0,3,1,4,2:T(8,128)(2,1)} copy(bf16[64,2,8,16,32]{4,3,2,1,0:T(8,128)(2,1)} %reshape.178) | data formatting | bytes 2097152 | tf_op jit(solution)/shard_map/reshape | solution.py:147
  115.7 4.0 %convolution_bitcast_fusion = f32[64,8,32,64]{0,3,2,1:T(8,128)S(1)} fusion(bf16[64,2,8,16,32]{0,3,1,4,2:T(8,128)(2,1)} %copy.69, f32[1,16,64]{2,1,0:T(8,128)S(1)} %get-tuple-element.51, f32[1,16,64]{2,1,0:T(8,128)S(1)} %get-tuple-element.50), kind=kOutput, calls=%fused_computation.27 | convolution fusion | flops 201328640 | bytes 5251072 | tf_op jit(solution)/shard_map/fagmn,ame->fgne/dot_general | solution.py:61
  119.7 9.7 %add_bitcast_fusion = (f32[64,8,1,32,32]{0,4,3,1,2:T(8,128)}, f32[64,8,1,32,32]{0,4,3,1,2:T(8,128)}, f32[64,8,1,32,32]{0,4,3,1,2:T(8,128)}, f32[64,8,1,32,32]{0,4,3,1,2:T(8,128)}) fusion(f32[64,8,32,64]{0,3,2,1:T(8,128)} %convolution_bitcast_fusion.1, f32[32,32]{1,0:T(8,128)S(1)} %get-tuple-element.56, f32[32,32]{1,0:T(8,128)S(1)} %get-tuple-element.57, ...), kind=kLoop, calls=%fused_computation.20 | loop fusion | flops 6291456 | bytes 16785408 | tf_op jit(solution)/shard_map/stack | solution.py:46
  129.4 4.5 %pad_maximum_fusion = f32[64,8,2,32,32]{0,4,3,1,2:T(8,128)S(1)} fusion(f32[64,8,1,32,32]{0,4,3,1,2:T(8,128)} %get-tuple-element.44, f32[64,8,1,32,32]{0,4,3,1,2:T(8,128)} %get-tuple-element.45), kind=kLoop, calls=%fused_computation | loop fusion | flops 1048576 | bytes 8388608 | tf_op jit(solution)/shard_map/stack | solution.py:46
  133.9 8.6 %fusion.12 = f32[64,8,32,64]{0,3,2,1:T(8,128)S(1)} fusion(f32[64,8,2,32,32]{0,4,3,1,2:T(8,128)S(1)} %pad_maximum_fusion, f32[1,32,64]{2,1,0:T(8,128)S(1)} %get-tuple-element.47, f32[1,32,64]{2,1,0:T(8,128)S(1)} %get-tuple-element.46), kind=kOutput, calls=%fused_computation.28 | convolution fusion | flops 402657280 | bytes 8404992 | tf_op jit(solution)/shard_map/...cnk,cne->...ke/dot_general | solution.py:51
  142.5 8.1 %pad_maximum_fusion.2 = f32[64,8,2,32,32]{0,4,3,1,2:T(8,128)} fusion(f32[64,8,1,32,32]{0,4,3,1,2:T(8,128)} %get-tuple-element.23, f32[64,8,1,32,32]{0,4,3,1,2:T(8,128)} %get-tuple-element.22), kind=kLoop, calls=%fused_computation.6 | loop fusion | flops 1048576 | bytes 8388608 | tf_op jit(solution)/shard_map/stack | solution.py:46
  150.6 12.3 %fusion.15 = f32[64,8,32,64]{0,3,2,1:T(8,128)S(1)} fusion(f32[64,8,2,32,32]{0,4,3,1,2:T(8,128)} %pad_maximum_fusion.2, f32[1,32,64]{2,1,0:T(8,128)S(1)} %get-tuple-element.47, f32[1,32,64]{2,1,0:T(8,128)S(1)} %get-tuple-element.46), kind=kOutput, calls=%fused_computation.29 | convolution fusion | flops 402657280 | bytes 8404992 | tf_op jit(solution)/shard_map/...cnk,cne->...ke/dot_general | solution.py:51
  163.0 5.5 %add_reduce_fusion = (f32[64,32,32]{0,2,1:T(8,128)}, f32[64,32,32]{0,2,1:T(8,128)}, f32[64,8,32,32]{0,3,2,1:T(8,128)}, f32[64,8,32,32]{0,3,2,1:T(8,128)}) fusion(f32[64,8,32,64]{0,3,2,1:T(8,128)S(1)} %fusion.15, f32[64,8,32,64]{0,3,2,1:T(8,128)S(1)} %fusion.12, f32[64,32,32]{0,2,1:T(8,128)S(1)} %copy-done.3, f32[64,32,32]{0,2,1:T(8,128)S(1)} %copy-done.2), kind=kLoop, calls=%fused_computation.18 | loop fusion | flops 7208960 | bytes 13631488 | tf_op jit(solution)/shard_map/reduce_sum | solution.py:157
  168.5 6.1 %fusion = f32[64,8,32,64]{0,3,2,1:T(8,128)S(1)} fusion(f32[64,8,32,32]{0,3,2,1:T(8,128)} %get-tuple-element.28, f32[64,8,32,32]{0,3,2,1:T(8,128)} %get-tuple-element.29, f32[32,32]{1,0:T(8,128)S(1)} %get-tuple-element.59, f32[32,32]{1,0:T(8,128)S(1)} %fusion.79, f32[32,32]{1,0:T(8,128)S(1)} %get-tuple-element.58), kind=kOutput, calls=%fused_computation.1 | convolution fusion | flops 403714048 | bytes 8400896 | tf_op jit(solution)/shard_map/...ke,ew->...kw/dot_general | solution.py:91
  174.7 2.6 subtract_bitcast_fusion.1
  177.3 3.4 %pad_maximum_fusion.1 = f32[64,8,2,32,32]{0,4,3,1,2:T(8,128)S(1)} fusion(f32[64,8,1,32,32]{0,4,3,1,2:T(8,128)} %get-tuple-element.25, f32[64,8,1,32,32]{0,4,3,1,2:T(8,128)S(1)} %get-tuple-element.24), kind=kLoop, calls=%fused_computation.5 | loop fusion | flops 1048576 | bytes 8388608 | tf_op jit(solution)/shard_map/stack | solution.py:95
  180.7 8.0 %multiply_reduce_fusion = (f32[64,2,8]{0,2,1:T(8,128)S(1)}, f32[64,2,8,16,32]{0,3,4,2,1:T(8,128)}) fusion(f32[64,2,8,16,32]{0,3,4,2,1:T(8,128)S(1)} %copy-done, f32[64,8,2,32,32]{0,4,3,1,2:T(8,128)S(1)} %pad_maximum_fusion.1, f32[1,16,2,32]{3,1,2,0:T(8,128)S(1)} %get-tuple-element.49, f32[1,16,2,32]{3,1,2,0:T(8,128)S(1)} %get-tuple-element.48), kind=kOutput, calls=%fused_computation.16 | convolution fusion | flops 202900480 | bytes 8400896 | tf_op jit(solution)/shard_map/dmck,...ckn->dm...n/dot_general | solution.py:109
  188.8 9.1 %copy.74 = f32[64,2,8,16,32]{4,3,2,1,0:T(8,128)} copy(f32[64,2,8,16,32]{0,3,4,2,1:T(8,128)} %get-tuple-element.53) | data formatting | bytes 4194304 | tf_op jit(solution)/shard_map/mul | solution.py:109
  197.9 7.3 %reshape.179 = f32[1024,512]{1,0:T(8,128)} reshape(f32[64,2,8,16,32]{4,3,2,1,0:T(8,128)} %copy.74) | data formatting | bytes 4194304 | tf_op jit(solution)/shard_map/reshape | solution.py:161
  205.2 14.0 %multiply_reduce_fusion.1 = (f32[1024]{0:T(1024)S(1)}, f32[1024]{0:T(1024)S(1)}, f32[1024]{0:T(1024)S(1)}, f32[1024]{0:T(1024)S(1)}, f32[1024]{0:T(1024)S(1)}, /...) fusion(f32[1024,512]{1,0:T(8,128)} %reshape.179, f32[1024,512]{1,0:T(8,128)S(1)} %copy.79, f32[1024]{0:T(1024)S(1)} %bitcast.175, ...), kind=kLoop, calls=%fused_computation.57 | loop fusion | flops 13625344 | bytes 5296128 | tf_op jit(solution)/shard_map/reduce_sum | solution.py:173
  220.5 5.1 %all-to-all-start.1 = ((bf16[1024,4,128]{0,2,1:T(8,128)(2,1)}), bf16[1024,4,128]{0,2,1:T(8,128)(2,1)S(1)}, u32[]{:S(2)}, u32[]{:S(2)}) async-start(bf16[1024,4,128]{0,2,1:T(8,128)(2,1)} %bitcast.49), calls=%async_computation.1 | async-start | bytes 2097152 | tf_op jit(solution)/shard_map/all_to_all | solution.py:182
  231.6 11.0 %psum.15 = f32[7,1024]{1,0:T(8,128)S(1)} all-reduce(f32[7,1024]{1,0:T(8,128)S(1)} %stack.151), channel_id=1, replica_groups=mesh['dp'=4,'pipe'=2,'ctx'=4] {'dp'}, use_global_device_ids=true, to_apply=%region_10.11 | all-reduce | flops 7168 | bytes 57344 | tf_op jit(solution)/shard_map/psum | solution.py:180
  243.2 21.9 %all-reduce.4.cloned.1.call-done = f32[64,512]{0,1:T(8,128)} async-done(((f32[64,512]{0,1:T(8,128)}), f32[64,512]{0,1:T(8,128)}) %all-reduce.4.cloned.1.call-update) | async-done | bytes 131088 | tf_op jit(solution)/shard_map/psum | solution.py:180
  (53 shorter events, 22.0 us)
Async XLA Ops:
  7.2 11.4 %copy-start.4 = (f32[1,64,512]{2,1,0:T(8,128)S(1)}, f32[1,64,512]{2,1,0:T(8,128)}, u32[]{:S(2)}) copy-start(f32[1,64,512]{2,1,0:T(8,128)} %param.7) | copy-start | bytes 393220
  9.5 33.5 %all-to-all-start.2 = ((bf16[4,1024,128]{2,1,0:T(8,128)(2,1)}), bf16[4,1024,128]{2,1,0:T(8,128)(2,1)S(1)}, u32[]{:S(2)}, u32[]{:S(2)}) async-start(bf16[4,1024,128]{2,1,0:T(8,128)(2,1)} %bitcast.57), calls=%async_computation.2 | async-start | bytes 2097152 | tf_op jit(solution)/shard_map/all_to_all | solution.py:133
  15.8 24.9 %collective-permute-start = (bf16[1,1,128,4096]{3,2,1,0:T(8,128)(2,1)}, bf16[1,1,128,4096]{3,2,1,0:T(8,128)(2,1)}, u32[]{:S(2)}, u32[]{:S(2)}) collective-permute-start(bf16[1,1,128,4096]{3,2,1,0:T(8,128)(2,1)} %param.4), channel_id=1, source_target_pairs={{0,4},{4,0},{1,5},{5,1},{2,6},{6,2},{3,7},{7,3},{8,12},{12,8},{9,1... | collective-permute-start | bytes 3145736 | tf_op jit(solution)/shard_map/ppermute | solution.py:14
  43.0 58.8 %all-to-all-start = ((bf16[4,1024,128]{2,1,0:T(8,128)(2,1)}), bf16[4,1024,128]{2,1,0:T(8,128)(2,1)}, u32[]{:S(2)}, u32[]{:S(2)}) async-start(bf16[4,1024,128]{2,1,0:T(8,128)(2,1)} %bitcast.23), calls=%async_computation | async-start | bytes 2097152 | tf_op jit(solution)/shard_map/all_to_all | solution.py:132
  150.6 12.3 %copy-start.2 = (f32[64,32,32]{0,2,1:T(8,128)S(1)}, f32[64,32,32]{0,2,1:T(8,128)}, u32[]{:S(2)}) copy-start(f32[64,32,32]{0,2,1:T(8,128)} %get-tuple-element.35) | copy-start | bytes 786436
  150.6 12.3 %copy-start.3 = (f32[64,32,32]{0,2,1:T(8,128)S(1)}, f32[64,32,32]{0,2,1:T(8,128)}, u32[]{:S(2)}) copy-start(f32[64,32,32]{0,2,1:T(8,128)} %get-tuple-element.36) | copy-start | bytes 786436
  177.3 3.5 %copy-start = (f32[64,2,8,16,32]{0,3,4,2,1:T(8,128)S(1)}, f32[64,2,8,16,32]{0,3,4,2,1:T(8,128)}, u32[]{:S(2)}) copy-start(f32[64,2,8,16,32]{0,3,4,2,1:T(8,128)} %copy.89) | copy-start | bytes 6291460
  219.2 6.7 %copy-start.1 = (f32[64,32,32]{0,2,1:T(8,128)S(1)}, f32[64,32,32]{0,2,1:T(8,128)}, u32[]{:S(2)}) copy-start(f32[64,32,32]{0,2,1:T(8,128)} %get-tuple-element.12) | copy-start | bytes 786436
  220.5 46.4 %all-to-all-start.1 = ((bf16[1024,4,128]{0,2,1:T(8,128)(2,1)}), bf16[1024,4,128]{0,2,1:T(8,128)(2,1)S(1)}, u32[]{:S(2)}, u32[]{:S(2)}) async-start(bf16[1024,4,128]{0,2,1:T(8,128)(2,1)} %bitcast.49), calls=%async_computation.1 | async-start | bytes 2097152 | tf_op jit(solution)/shard_map/all_to_all | solution.py:182
  225.6 39.5 %all-reduce.4.cloned.1.call-start = ((), (), s32[]{:S(2)}) async-start(), calls=%async_computation.3 | async-start | bytes 524288 | tf_op jit(solution)/shard_map/psum | solution.py:180
Sparse Core Ops, SparseCore 0:
  231.7 33.4 all-reduce.3
where the time goes:
time: 279 us; the launch traced here: 276 us
  local copies, waits for them, and re-layouts  81.2 us (29%)
  other arithmetic  56 us (20%)
  matrix products  52.5 us (19%)
  waiting for transfers between devices  42.6 us (15%)
  starting transfers between devices  18 us (6%)
  between operations  14.6 us (5%)
  blocking collectives  11 us (4%)
    another operation x5, other arithmetic, finish_forward(): jnp.stack([first_re * cos_turn + first_im * sin_turn, first_im * cos_turn...  22.7 us
    dot_general x3, matrix products, finish_forward(): jnp.einsum('...cnk,cne->...ke', turned, block_table(cos_last, sin_last),...  22.1 us
    convert_element_type x5, local copies, waits for them, and re-layouts, body(): feature_vals = feature_block.astype(jnp.float32)  21.9 us
    psum x1, waiting for transfers between devices, body(): filter_total, tap_total = lax.psum((filter_part, tap_part), 'dp')  21.9 us
    ppermute x1, waiting for transfers between devices, passed_along(): return lax.ppermute(value, axis, pairs)  20.7 us
    reshape x2, local copies, waits for them, and re-layouts, body(): spectrum_u = forward_pairs(conv_in.reshape(pair_shape))  14.9 us
    reduce_sum x1, other arithmetic, body(): jnp.sum(conv_in_grad * padded_feat[:, taps_count - 1 - offset:taps_count...  14 us
    dot_general x2, matrix products, forward_pairs(): jnp.einsum('fagmn,ame->fgne', values, block_table(cos_first, sin_first),...  12.9 us
  transfers between devices with their start and end apart: 5, of which 2 were waited for; matrix products, arithmetic and copies ran while one was open for 24% of the time, Pallas kernels for 0%

commit v1 on v0

--- a/solution.py
+++ b/solution.py
@@ -1,11 +1,15 @@
+import functools
 import math
 
 import jax
 import jax.numpy as jnp
 from jax import lax
+from jax.experimental import pallas as pl
+from jax.experimental.pallas import tpu as pltpu
 from jax.sharding import PartitionSpec as P
 
 TABLE_PRECISION = lax.Precision.HIGH
+MESH = pl.DeviceIdType.MESH
 
 
 def passed_along(value, axis, steps):
@@ -188,6 +192,335 @@
     return (feature_grads, filter_grads, tap_grads)
 
 
+def fused_kernel(
+    sizes,
+    arriving,
+    features,
+    taps,
+    filters,
+    feature_out,
+    filter_out,
+    tap_out,
+    inbox,
+    outbox,
+    shares,
+    wide_feat,
+    split_in,
+    pair_grad,
+    twin_grad,
+    conv_grad,
+    diagonals,
+    send_in,
+    recv_in,
+    send_out,
+    recv_out,
+    send_share,
+    recv_share,
+):
+    blocks, dp_count, pipe_count, chunks, rows, width, group, taps_count = sizes
+    seq_len = blocks * rows
+    own_width = chunks * width
+    per_chunk = width // group
+    me = lax.axis_index("ctx")
+    dp_rank = lax.axis_index("dp")
+    pipe_rank = lax.axis_index("pipe")
+    before = lax.rem(pipe_rank + pipe_count - 1, pipe_count)
+
+    barrier = pltpu.get_barrier_semaphore()
+    for step in range(1, blocks):
+        pl.semaphore_signal(
+            barrier,
+            inc=1,
+            device_id={"ctx": lax.rem(me + step, blocks)},
+            device_id_type=MESH,
+        )
+    for step in range(blocks):
+        pl.semaphore_signal(
+            barrier,
+            inc=1,
+            device_id={"pipe": before, "ctx": lax.rem(me + step, blocks)},
+            device_id_type=MESH,
+        )
+    for step in range(1, dp_count):
+        pl.semaphore_signal(
+            barrier,
+            inc=1,
+            device_id={"dp": lax.rem(dp_rank + step, dp_count)},
+            device_id_type=MESH,
+        )
+    pl.semaphore_wait(barrier, 2 * blocks + dp_count - 2)
+
+    def columns(owner, chunk):
+        return pl.ds(pl.multiple_of(owner * own_width + chunk * width, width), width)
+
+    def send_chunk(chunk, carry):
+        for step in range(blocks):
+            target = lax.rem(me + step, blocks)
+            pltpu.make_async_remote_copy(
+                src_ref=arriving.at[:, columns(target, chunk)],
+                dst_ref=inbox.at[chunk, blocks + me],
+                send_sem=send_in,
+                recv_sem=recv_in.at[chunk],
+                device_id={"pipe": before, "ctx": target},
+                device_id_type=MESH,
+            ).start()
+            if step:
+                pltpu.make_async_remote_copy(
+                    src_ref=features.at[:, columns(target, chunk)],
+                    dst_ref=inbox.at[chunk, me],
+                    send_sem=send_in,
+                    recv_sem=recv_in.at[chunk],
+                    device_id={"ctx": target},
+                    device_id_type=MESH,
+                ).start()
+        pltpu.make_async_copy(
+            features.at[:, columns(me, chunk)], inbox.at[chunk, me], recv_in.at[chunk]
+        ).start()
+        return carry
+
+    lax.fori_loop(0, chunks, send_chunk, 0)
+
+    wide_feat[0:8, :] = jnp.zeros((8, width), jnp.float32)
+    conv_grad[seq_len : seq_len + 8, :] = jnp.zeros((8, width), jnp.float32)
+    row_index = lax.broadcasted_iota(jnp.int32, (rows, rows), 0)
+    lane_index = lax.broadcasted_iota(jnp.int32, (rows, rows), 1)
+    upper = lane_index >= row_index
+    lane_group = lane_index // group
+    zero_tile = jnp.zeros((rows, rows), jnp.float32)
+
+    def do_chunk(chunk, carry):
+        pltpu.make_async_copy(inbox.at[chunk], inbox.at[chunk], recv_in.at[chunk]).wait()
+        tap_rows = taps[:, columns(me, chunk)]
+        for block in range(blocks):
+            wide_feat[8 + block * rows : 8 + (block + 1) * rows, :] = inbox[chunk, block].astype(
+                jnp.float32
+            )
+        for block in range(blocks):
+            here = slice(block * rows, (block + 1) * rows)
+            summed = zero_tile
+            for tap in range(taps_count):
+                start = 8 + block * rows - tap
+                summed = summed + tap_rows[tap : tap + 1] * wide_feat[start : start + rows, :]
+            high = summed.astype(jnp.bfloat16)
+            low = (summed - high.astype(jnp.float32)).astype(jnp.bfloat16)
+            split_in[here, 0:width] = high
+            split_in[here, width : 2 * width] = low
+            grad = inbox[chunk, blocks + block]
+            twin_grad[here, 0:width] = grad
+            twin_grad[here, width : 2 * width] = grad
+            pair_grad[here, 0:width] = grad
+            if block:
+                pair_grad[(block - 1) * rows : block * rows, width : 2 * width] = grad
+        pair_grad[seq_len - rows : seq_len, width : 2 * width] = jnp.zeros(
+            (rows, width), jnp.bfloat16
+        )
+
+        def do_filter(index, inner):
+            ours = lane_group == index
+            kernel_row = filters[pl.ds(chunk * per_chunk + index, 1), :]
+            highs, lows = [], []
+            last = zero_tile
+            for block in range(blocks):
+                spread = jnp.broadcast_to(
+                    kernel_row[:, block * rows : (block + 1) * rows], (rows, rows)
+                )
+                rolled = pltpu.roll(spread, 0, 1, stride=1, stride_axis=0)
+                tile = jnp.where(upper, rolled, last)
+                last = rolled
+                high = tile.astype(jnp.bfloat16)
+                highs.append(high)
+                lows.append((tile - high.astype(jnp.float32)).astype(jnp.bfloat16))
+            table = jnp.concatenate(
+                [jnp.concatenate(highs, axis=1), jnp.concatenate(lows, axis=1)], axis=0
+            )
+            for block in range(0, blocks, 2):
+                product = jnp.dot(
+                    table[:, : seq_len - block * rows],
+                    pair_grad[block * rows :, :],
+                    preferred_element_type=jnp.float32,
+                )
+                both = product[:rows] + product[rows:]
+                for half in range(2):
+                    here = slice((block + half) * rows, (block + half + 1) * rows)
+                    conv_grad[here, :] = jnp.where(
+                        ours, both[:, half * width : (half + 1) * width], conv_grad[here, :]
+                    )
+            ours_twice = jnp.concatenate([ours, ours], axis=1)
+            picked = [
+                jnp.where(
+                    ours_twice,
+                    split_in[block * rows : (block + 1) * rows, :],
+                    jnp.zeros((rows, 2 * width), jnp.bfloat16),
+                )
+                for block in range(blocks)
+            ]
+            sums = [None] * blocks
+            for block in range(0, blocks, 2):
+                product = lax.dot_general(
+                    jnp.concatenate(picked[: block + 2], axis=0),
+                    twin_grad[block * rows : (block + 2) * rows, :],
+                    (((1,), (1,)), ((), ())),
+                    preferred_element_type=jnp.float32,
+                )
+                for half in range(2):
+                    for early in range(block + half + 1):
+                        lag = block + half - early
+                        piece = product[
+                            early * rows : (early + 1) * rows, half * rows : (half + 1) * rows
+                        ]
+                        sums[lag] = piece if sums[lag] is None else sums[lag] + piece
+            for lag in range(blocks):
+                following = sums[lag + 1] if lag + 1 < blocks else zero_tile
+                merged = jnp.where(upper, sums[lag], following)
+                folded = merged[0:8]
+                for part in range(1, rows // 8):
+                    folded = folded + pltpu.roll(
+                        merged[part * 8 : part * 8 + 8], rows - part * 8, 1
+                    )
+                place = pl.multiple_of((lag * per_chunk + index) * 8, 8)
+                diagonals[pl.ds(place, 8), :] = folded
+            return inner
+
+        lax.fori_loop(0, per_chunk, do_filter, 0)
+
+        lagged = diagonals[pl.ds(0, blocks * per_chunk, stride=8), :]
+        for turn in range(1, 8):
+            lagged = lagged + pltpu.roll(
+                diagonals[pl.ds(turn, blocks * per_chunk, stride=8), :], rows - turn, 1
+            )
+        for lag in range(blocks):
+            shares[dp_rank, chunk, :, lag * rows : (lag + 1) * rows] = lagged[
+                lag * per_chunk : (lag + 1) * per_chunk
+            ]
+        tap_sums = [jnp.zeros((1, width), jnp.float32)] * taps_count
+        for block in range(blocks):
+            here = block * rows
+            summed = zero_tile
+            grads = conv_grad[here : here + rows, :]
+            for tap in range(taps_count):
+                summed = summed + tap_rows[tap : tap + 1] * conv_grad[here + tap : here + tap + rows, :]
+                start = 8 + here - tap
+                tap_sums[tap] = tap_sums[tap] + jnp.sum(
+                    grads * wide_feat[start : start + rows, :], axis=0, keepdims=True
+                )
+            outbox[chunk, block] = summed.astype(jnp.bfloat16)
+        filler = [jnp.zeros((per_chunk - taps_count, width), jnp.float32)]
+        shares[dp_rank, chunk, :, seq_len : seq_len + width] = jnp.concatenate(
+            tap_sums + (filler if per_chunk > taps_count else []), axis=0
+        )
+        for step in range(1, blocks):
+            target = lax.rem(me + step, blocks)
+            pltpu.make_async_remote_copy(
+                src_ref=outbox.at[chunk, target],
+                dst_ref=feature_out.at[:, columns(me, chunk)],
+                send_sem=send_out,
+                recv_sem=recv_out,
+                device_id={"ctx": target},
+                device_id_type=MESH,
+            ).start()
+        pltpu.make_async_copy(
+            outbox.at[chunk, me], feature_out.at[:, columns(me, chunk)], recv_out
+        ).start()
+        for step in range(1, dp_count):
+            pltpu.make_async_remote_copy(
+                src_ref=shares.at[dp_rank, chunk],
+                dst_ref=shares.at[dp_rank, chunk],
+                send_sem=send_share,
+                recv_sem=recv_share,
+                device_id={"dp": lax.rem(dp_rank + step, dp_count)},
+                device_id_type=MESH,
+            ).start()
+        return carry
+
+    lax.fori_loop(0, chunks, do_chunk, 0)
+
+    others = shares.at[0 : dp_count - 1]
+    pltpu.make_async_copy(others, others, recv_share).wait()
+    pltpu.make_async_copy(others, others, send_share).wait()
+    filter_scale = 1.0 / math.sqrt(dp_count * group * seq_len)
+    tap_scale = 1.0 / math.sqrt(dp_count * seq_len)
+    for chunk in range(chunks):
+        total = shares[0, chunk]
+        for rank in range(1, dp_count):
+            total = total + shares[rank, chunk]
+        filter_out[chunk * per_chunk : (chunk + 1) * per_chunk, :] = (
+            total[:, :seq_len] * filter_scale
+        )
+        tap_out[:, chunk * width : (chunk + 1) * width] = (
+            total[:taps_count, seq_len:] * tap_scale
+        )
+    inputs_sent = inbox.at[:, 0 : 2 * blocks - 1]
+    pltpu.make_async_copy(inputs_sent, inputs_sent, send_in).wait()
+    outputs_sent = outbox.at[:, 0 : blocks - 1]
+    pltpu.make_async_copy(outputs_sent, outputs_sent, send_out).wait()
+    pltpu.make_async_copy(outbox, outbox, recv_out).wait()
+
+
+def fused_body(arriving, features, short_taps, filters):
+    blocks = lax.axis_size("ctx")
+    dp_count = lax.axis_size("dp")
+    pipe_count = lax.axis_size("pipe")
+    rows, channels = features.shape[2], features.shape[3]
+    own_width = channels // blocks
+    filter_count, seq_len = filters.shape[1], filters.shape[2]
+    group = own_width // filter_count
+    taps_count = short_taps.shape[1]
+    width = rows
+    chunks = own_width // width
+    per_chunk = width // group
+    sizes = (blocks, dp_count, pipe_count, chunks, rows, width, group, taps_count)
+    anywhere = pl.BlockSpec(memory_space=pl.ANY)
+    vmem = pl.BlockSpec(memory_space=pltpu.VMEM)
+    feature_grads, filter_grads, tap_grads = pl.pallas_call(
+        functools.partial(fused_kernel, sizes),
+        out_shape=(
+            jax.ShapeDtypeStruct((rows, channels), jnp.bfloat16),
+            jax.ShapeDtypeStruct((filter_count, seq_len), jnp.float32),
+            jax.ShapeDtypeStruct((taps_count, own_width), jnp.float32),
+        ),
+        in_specs=[anywhere, anywhere, vmem, vmem],
+        out_specs=(anywhere, vmem, vmem),
+        scratch_shapes=[
+            pltpu.VMEM((chunks, 2 * blocks, rows, width), jnp.bfloat16),
+            pltpu.VMEM((chunks, blocks, rows, width), jnp.bfloat16),
+            pltpu.VMEM((dp_count, chunks, per_chunk, seq_len + width), jnp.float32),
+            pltpu.VMEM((seq_len + 8, width), jnp.float32),
+            pltpu.VMEM((seq_len, 2 * width), jnp.bfloat16),
+            pltpu.VMEM((seq_len, 2 * width), jnp.bfloat16),
+            pltpu.VMEM((seq_len, 2 * width), jnp.bfloat16),
+            pltpu.VMEM((seq_len + 8, width), jnp.float32),
+            pltpu.VMEM((blocks * per_chunk * 8, width), jnp.float32),
+            pltpu.SemaphoreType.DMA,
+            pltpu.SemaphoreType.DMA((chunks,)),
+            pltpu.SemaphoreType.DMA,
+            pltpu.SemaphoreType.DMA,
+            pltpu.SemaphoreType.DMA,
+            pltpu.SemaphoreType.DMA,
+        ],
+        compiler_params=pltpu.CompilerParams(
+            collective_id=0, has_side_effects=True, vmem_limit_bytes=32 * 1024 * 1024
+        ),
+    )(arriving[0, 0], features[0, 0], short_taps[0], filters[0])
+    return (feature_grads[None, None], filter_grads[None], tap_grads[None])
+
+
+def fits_fused(mesh, features, short_taps, filters):
+    blocks, rows = mesh.shape["ctx"], features.shape[2] // mesh.shape["ctx"]
+    own_width = features.shape[3] // blocks
+    own_filters = filters.shape[1] // blocks
+    group = own_width // own_filters
+    return (
+        rows == 128
+        and blocks % 2 == 0
+        and blocks <= 8
+        and mesh.shape["pipe"] == 2
+        and own_width % rows == 0
+        and rows % group == 0
+        and rows // group == 8
+        and short_taps.shape[1] <= 8
+    )
+
+
 def solution(mesh):
     in_specs = (
         P("pipe", "dp", "ctx", None),
@@ -196,4 +529,11 @@
         P("pipe", "ctx", None),
     )
     out_specs = (P("pipe", "dp", "ctx", None), P("pipe", "ctx", None), P("pipe", None, "ctx"))
-    return jax.shard_map(body, mesh=mesh, in_specs=in_specs, out_specs=out_specs, check_vma=False)
+
+    def run(arriving, features, short_taps, filters):
+        chosen = fused_body if fits_fused(mesh, features, short_taps, filters) else body
+        return jax.shard_map(
+            chosen, mesh=mesh, in_specs=in_specs, out_specs=out_specs, check_vma=False
+        )(arriving, features, short_taps, filters)
+
+    return run

time: 279 us -> 80.8 us (0.29)
  local copies, waits for them, and re-layouts: 81.2 us -> 5.72 us
  Pallas kernels: 0 us -> 74.2 us
  other arithmetic: 56 us -> 0 us
  matrix products: 52.5 us -> 0 us
  waiting for transfers between devices: 42.6 us -> 0 us
  starting transfers between devices: 18 us -> 0 us
  between operations: 14.6 us -> 0.67 us
  blocking collectives: 11 us -> 0 us
    pallas_call x0 -> x1, Pallas kernels: none -> 74.2 us  [fused_body(): pl.pallas_call(functools.partial(fused_kernel, sizes), out_shape=(jax.Sha...]
    dot_general x10 -> x0, matrix products: 52.5 us -> none  [the longest x3 22.1 us: finish_forward(): jnp.einsum('...cnk,cne->...ke', turned, block_table(cos_last, sin_last),...]
    reshape x5 -> x0, local copies, waits for them, and re-layouts: 34 us -> none  [the longest x2 14.9 us: body(): spectrum_u = forward_pairs(conv_in.reshape(pair_shape))]
    another operation x12 -> x0, other arithmetic: 29.3 us -> none  [the longest x5 22.7 us: finish_forward(): jnp.stack([first_re * cos_turn + first_im * sin_turn, first_im * cos_turn...]
    convert_element_type x6 -> x0, local copies, waits for them, and re-layouts: 23.3 us -> none  [the longest x5 21.9 us: body(): feature_vals = feature_block.astype(jnp.float32)]
    psum x1 -> x0, waiting for transfers between devices: 21.9 us -> none  [body(): filter_total, tap_total = lax.psum((filter_part, tap_part), 'dp')]
    ppermute x1 -> x0, waiting for transfers between devices: 20.7 us -> none  [passed_along(): return lax.ppermute(value, axis, pairs)]
    reduce_sum x2 -> x0, other arithmetic: 19.5 us -> none  [the longest x1 14 us: body(): jnp.sum(conv_in_grad * padded_feat[:, taps_count - 1 - offset:taps_count...]
  transfers between devices with their start and end apart: 5 -> 0, of which waited for: 2 -> 0; matrix products, arithmetic and copies ran while one was open for 24% -> 0% of each run, Pallas kernels for 0% -> 0%
where the time goes in v1:
time: 80.8 us; the launch traced here: 80.5 us
  Pallas kernels  74.2 us (92%)
  local copies, waits for them, and re-layouts  5.72 us (7%)
    pallas_call x1, Pallas kernels, fused_body(): pl.pallas_call(functools.partial(fused_kernel, sizes), out_shape=(jax.Sha...  74.2 us
    unnamed x10, local copies, waits for them, and re-layouts  5.72 us

profile of v1, /device:TPU:0, one launch (start us, length us, event | category | flops | bytes accessed | tf_op | source)
XLA Modules:
  0.0 80.5 jit_solution(75934934158129688)
XLA Ops:
  0.6 0.0 copy-start.2
  0.6 1.0 %copy.10 = f32[1,7,4096]{2,1,0:T(8,128)S(1)} copy(f32[1,7,4096]{2,0,1:T(1,128)} %param.6) | data formatting | bytes 229376
  1.6 0.0 copy-done.2
  1.7 0.0 copy-start
  1.7 1.2 %copy-done = bf16[1,1,128,4096]{3,2,1,0:T(8,128)(2,1)S(1)} copy-done((bf16[1,1,128,4096]{3,2,1,0:T(8,128)(2,1)S(1)}, bf16[1,1,128,4096]{3,2,1,0:T(8,128)(2,1)}, u32[]{:S(2)}) %copy-start) | copy-done | bytes 1048600
  2.9 0.0 copy-start.1
  2.9 1.2 %copy-done.1 = bf16[1,1,128,4096]{3,2,1,0:T(8,128)(2,1)S(1)} copy-done((bf16[1,1,128,4096]{3,2,1,0:T(8,128)(2,1)S(1)}, bf16[1,1,128,4096]{3,2,1,0:T(8,128)(2,1)}, u32[]{:S(2)}) %copy-start.1) | copy-done | bytes 1048600
  4.1 74.2 %shard_map.67 = (bf16[128,4096]{1,0:T(8,128)(2,1)S(1)}, f32[64,512]{1,0:T(8,128)S(1)}, f32[7,1024]{1,0:T(8,128)S(1)}) custom-call(bf16[128,4096]{1,0:T(8,128)(2,1)S(1)} %bitcast.9, bf16[128,4096]{1,0:T(8,128)(2,1)S(1)} %bitcast.10, f32[7,4096]{1,0:T(8,128)S(1)} %bitcast.12, f32[64,512]{1,0:T(8,128)S(1)} %bitcast.13), custom_call_target="tpu_custom_call" | custom-call | tf_op jit(solution)/shard_map/pallas_call | solution.py:474
  78.3 0.6 copy.7
  78.9 1.0 %copy.13 = bf16[1,1,128,4096]{3,2,1,0:T(8,128)(2,1)} copy(bf16[1,1,128,4096]{3,2,1,0:T(8,128)(2,1)S(1)} %bitcast.11) | data formatting | bytes 2097152
  79.9 0.7 copy.14
Async XLA Ops:
  0.6 1.0 %copy-start.2 = (f32[1,64,512]{2,1,0:T(8,128)S(1)}, f32[1,64,512]{2,1,0:T(8,128)}, u32[]{:S(2)}) copy-start(f32[1,64,512]{2,1,0:T(8,128)} %param.7) | copy-start | bytes 393220
  1.7 1.2 %copy-start = (bf16[1,1,128,4096]{3,2,1,0:T(8,128)(2,1)S(1)}, bf16[1,1,128,4096]{3,2,1,0:T(8,128)(2,1)}, u32[]{:S(2)}) copy-start(bf16[1,1,128,4096]{3,2,1,0:T(8,128)(2,1)} %param.4) | copy-start | bytes 3145732
  2.9 1.2 %copy-start.1 = (bf16[1,1,128,4096]{3,2,1,0:T(8,128)(2,1)S(1)}, bf16[1,1,128,4096]{3,2,1,0:T(8,128)(2,1)}, u32[]{:S(2)}) copy-start(bf16[1,1,128,4096]{3,2,1,0:T(8,128)(2,1)} %param.5) | copy-start | bytes 3145732

commit v2 on v1

--- a/solution.py
+++ b/solution.py
@@ -196,22 +196,38 @@
     sizes,
     arriving,
     features,
-    taps,
-    filters,
+    taps_all,
+    filters_all,
     feature_out,
     filter_out,
     tap_out,
+    taps,
+    filters,
+    lent_filters,
     inbox,
+    late_inbox,
+    late_edge,
     outbox,
+    late_outbox,
     shares,
+    late_share,
+    late_landed,
     wide_feat,
     split_in,
     pair_grad,
     twin_grad,
     conv_grad,
     diagonals,
+    local_sems,
     send_in,
     recv_in,
+    recv_late,
+    send_edge,
+    recv_edge,
+    send_lent,
+    recv_lent,
+    send_late,
+    recv_landed,
     send_out,
     recv_out,
     send_share,
@@ -219,12 +235,20 @@
 ):
     blocks, dp_count, pipe_count, chunks, rows, width, group, taps_count = sizes
     seq_len = blocks * rows
+    half = blocks // 2
     own_width = chunks * width
     per_chunk = width // group
     me = lax.axis_index("ctx")
     dp_rank = lax.axis_index("dp")
     pipe_rank = lax.axis_index("pipe")
     before = lax.rem(pipe_rank + pipe_count - 1, pipe_count)
+    is_early = me < half
+    is_late = me >= half
+
+    fetch_taps = pltpu.make_async_copy(taps_all, taps, local_sems.at[0])
+    fetch_taps.start()
+    fetch_filters = pltpu.make_async_copy(filters_all.at[0], filters, local_sems.at[1])
+    fetch_filters.start()
 
     barrier = pltpu.get_barrier_semaphore()
     for step in range(1, blocks):
@@ -253,74 +277,138 @@
     def columns(owner, chunk):
         return pl.ds(pl.multiple_of(owner * own_width + chunk * width, width), width)
 
+    def tap_rows_of(owner, chunk):
+        place = owner * chunks + chunk
+        return [taps[tap, pl.ds(place, 1), :] for tap in range(taps_count)]
+
+    def send(source, target, send_sem, recv_sem, device):
+        pltpu.make_async_remote_copy(
+            src_ref=source,
+            dst_ref=target,
+            send_sem=send_sem,
+            recv_sem=recv_sem,
+            device_id=device,
+            device_id_type=MESH,
+        ).start()
+
     def send_chunk(chunk, carry):
+        @pl.when(is_early)
+        def _():
+            send(
+                filters_all.at[0, pl.ds(pl.multiple_of(chunk * per_chunk, 8), per_chunk), 0 : half * rows],
+                lent_filters.at[chunk],
+                send_lent,
+                recv_lent.at[chunk],
+                {"ctx": me + half},
+            )
+
+        @pl.when(me == half - 1)
+        def _():
+            for owner in range(half):
+                send(
+                    features.at[rows - 16 : rows, columns(owner, chunk)],
+                    late_edge.at[chunk],
+                    send_edge,
+                    recv_edge.at[chunk],
+                    {"ctx": half + owner},
+                )
+
+        @pl.when(is_late)
+        def _():
+            for step in range(half):
+                owner = lax.rem(me + step, half)
+                device = owner + half
+                send(
+                    arriving.at[:, columns(owner, chunk)],
+                    late_inbox.at[chunk, me - half],
+                    send_in,
+                    recv_late.at[chunk],
+                    {"pipe": before, "ctx": device},
+                )
+                if step:
+                    send(
+                        features.at[:, columns(owner, chunk)],
+                        late_inbox.at[chunk, me],
+                        send_in,
+                        recv_late.at[chunk],
+                        {"ctx": device},
+                    )
+                else:
+                    pltpu.make_async_copy(
+                        features.at[:, columns(owner, chunk)],
+                        late_inbox.at[chunk, me],
+                        recv_late.at[chunk],
+                    ).start()
+
         for step in range(blocks):
             target = lax.rem(me + step, blocks)
-            pltpu.make_async_remote_copy(
-                src_ref=arriving.at[:, columns(target, chunk)],
-                dst_ref=inbox.at[chunk, blocks + me],
-                send_sem=send_in,
-                recv_sem=recv_in.at[chunk],
-                device_id={"pipe": before, "ctx": target},
-                device_id_type=MESH,
-            ).start()
+            send(
+                arriving.at[:, columns(target, chunk)],
+                inbox.at[chunk, me],
+                send_in,
+                recv_in.at[chunk],
+                {"pipe": before, "ctx": target},
+            )
             if step:
-                pltpu.make_async_remote_copy(
-                    src_ref=features.at[:, columns(target, chunk)],
-                    dst_ref=inbox.at[chunk, me],
-                    send_sem=send_in,
-                    recv_sem=recv_in.at[chunk],
-                    device_id={"ctx": target},
-                    device_id_type=MESH,
-                ).start()
+
+                @pl.when(jnp.logical_or(is_early, target >= half))
+                def _():
+                    send(
+                        features.at[:, columns(target, chunk)],
+                        inbox.at[chunk, blocks + me],
+                        send_in,
+                        recv_in.at[chunk],
+                        {"ctx": target},
+                    )
+
         pltpu.make_async_copy(
-            features.at[:, columns(me, chunk)], inbox.at[chunk, me], recv_in.at[chunk]
+            features.at[:, columns(me, chunk)], inbox.at[chunk, blocks + me], recv_in.at[chunk]
         ).start()
         return carry
 
     lax.fori_loop(0, chunks, send_chunk, 0)
-
-    wide_feat[0:8, :] = jnp.zeros((8, width), jnp.float32)
-    conv_grad[seq_len : seq_len + 8, :] = jnp.zeros((8, width), jnp.float32)
+    fetch_taps.wait()
+    fetch_filters.wait()
+
     row_index = lax.broadcasted_iota(jnp.int32, (rows, rows), 0)
     lane_index = lax.broadcasted_iota(jnp.int32, (rows, rows), 1)
     upper = lane_index >= row_index
     lane_group = lane_index // group
     zero_tile = jnp.zeros((rows, rows), jnp.float32)
 
-    def do_chunk(chunk, carry):
-        pltpu.make_async_copy(inbox.at[chunk], inbox.at[chunk], recv_in.at[chunk]).wait()
-        tap_rows = taps[:, columns(me, chunk)]
-        for block in range(blocks):
-            wide_feat[8 + block * rows : 8 + (block + 1) * rows, :] = inbox[chunk, block].astype(
+    def convolve(tap_rows, feat_at, grad_at, kernel_at, feat_blocks, grad_blocks):
+        for block in range(feat_blocks):
+            wide_feat[8 + block * rows : 8 + (block + 1) * rows, :] = feat_at(block).astype(
                 jnp.float32
             )
-        for block in range(blocks):
+        for block in range(feat_blocks):
             here = slice(block * rows, (block + 1) * rows)
             summed = zero_tile
             for tap in range(taps_count):
                 start = 8 + block * rows - tap
-                summed = summed + tap_rows[tap : tap + 1] * wide_feat[start : start + rows, :]
+                summed = summed + tap_rows[tap] * wide_feat[start : start + rows, :]
             high = summed.astype(jnp.bfloat16)
             low = (summed - high.astype(jnp.float32)).astype(jnp.bfloat16)
             split_in[here, 0:width] = high
             split_in[here, width : 2 * width] = low
-            grad = inbox[chunk, blocks + block]
+        for block in range(grad_blocks):
+            here = slice(block * rows, (block + 1) * rows)
+            grad = grad_at(block)
             twin_grad[here, 0:width] = grad
             twin_grad[here, width : 2 * width] = grad
             pair_grad[here, 0:width] = grad
             if block:
                 pair_grad[(block - 1) * rows : block * rows, width : 2 * width] = grad
-        pair_grad[seq_len - rows : seq_len, width : 2 * width] = jnp.zeros(
+        pair_grad[(grad_blocks - 1) * rows : grad_blocks * rows, width : 2 * width] = jnp.zeros(
             (rows, width), jnp.bfloat16
         )
 
         def do_filter(index, inner):
             ours = lane_group == index
-            kernel_row = filters[pl.ds(chunk * per_chunk + index, 1), :]
+            kernel_row = kernel_at(index)
             highs, lows = [], []
             last = zero_tile
-            for block in range(blocks):
+            for block in range(grad_blocks):
                 spread = jnp.broadcast_to(
                     kernel_row[:, block * rows : (block + 1) * rows], (rows, rows)
                 )
@@ -333,17 +421,17 @@
             table = jnp.concatenate(
                 [jnp.concatenate(highs, axis=1), jnp.concatenate(lows, axis=1)], axis=0
             )
-            for block in range(0, blocks, 2):
+            for block in range(0, feat_blocks, 2):
                 product = jnp.dot(
-                    table[:, : seq_len - block * rows],
-                    pair_grad[block * rows :, :],
+                    table[:, : (grad_blocks - block) * rows],
+                    pair_grad[block * rows : grad_blocks * rows, :],
                     preferred_element_type=jnp.float32,
                 )
                 both = product[:rows] + product[rows:]
-                for half in range(2):
-                    here = slice((block + half) * rows, (block + half + 1) * rows)
+                for side in range(2):
+                    here = slice((block + side) * rows, (block + side + 1) * rows)
                     conv_grad[here, :] = jnp.where(
-                        ours, both[:, half * width : (half + 1) * width], conv_grad[here, :]
+                        ours, both[:, side * width : (side + 1) * width], conv_grad[here, :]
                     )
             ours_twice = jnp.concatenate([ours, ours], axis=1)
             picked = [
@@ -352,25 +440,25 @@
                     split_in[block * rows : (block + 1) * rows, :],
                     jnp.zeros((rows, 2 * width), jnp.bfloat16),
                 )
-                for block in range(blocks)
+                for block in range(feat_blocks)
             ]
-            sums = [None] * blocks
-            for block in range(0, blocks, 2):
+            sums = [None] * grad_blocks
+            for block in range(0, grad_blocks, 2):
                 product = lax.dot_general(
                     jnp.concatenate(picked[: block + 2], axis=0),
                     twin_grad[block * rows : (block + 2) * rows, :],
                     (((1,), (1,)), ((), ())),
                     preferred_element_type=jnp.float32,
                 )
-                for half in range(2):
-                    for early in range(block + half + 1):
-                        lag = block + half - early
+                for side in range(2):
+                    for early in range(min(feat_blocks, block + side + 1)):
+                        lag = block + side - early
                         piece = product[
-                            early * rows : (early + 1) * rows, half * rows : (half + 1) * rows
+                            early * rows : (early + 1) * rows, side * rows : (side + 1) * rows
                         ]
                         sums[lag] = piece if sums[lag] is None else sums[lag] + piece
-            for lag in range(blocks):
-                following = sums[lag + 1] if lag + 1 < blocks else zero_tile
+            for lag in range(grad_blocks):
+                following = sums[lag + 1] if lag + 1 < grad_blocks else zero_tile
                 merged = jnp.where(upper, sums[lag], following)
                 folded = merged[0:8]
                 for part in range(1, rows // 8):
@@ -382,61 +470,166 @@
             return inner
 
         lax.fori_loop(0, per_chunk, do_filter, 0)
-
-        lagged = diagonals[pl.ds(0, blocks * per_chunk, stride=8), :]
+        count = grad_blocks * per_chunk
+        lagged = diagonals[pl.ds(0, count, stride=8), :]
         for turn in range(1, 8):
             lagged = lagged + pltpu.roll(
-                diagonals[pl.ds(turn, blocks * per_chunk, stride=8), :], rows - turn, 1
+                diagonals[pl.ds(turn, count, stride=8), :], rows - turn, 1
             )
-        for lag in range(blocks):
-            shares[dp_rank, chunk, :, lag * rows : (lag + 1) * rows] = lagged[
-                lag * per_chunk : (lag + 1) * per_chunk
-            ]
+        return [
+            lagged[lag * per_chunk : (lag + 1) * per_chunk] for lag in range(grad_blocks)
+        ]
+
+    def finish(tap_rows, feat_blocks, put):
         tap_sums = [jnp.zeros((1, width), jnp.float32)] * taps_count
-        for block in range(blocks):
+        for block in range(feat_blocks):
             here = block * rows
             summed = zero_tile
             grads = conv_grad[here : here + rows, :]
             for tap in range(taps_count):
-                summed = summed + tap_rows[tap : tap + 1] * conv_grad[here + tap : here + tap + rows, :]
+                summed = (
+                    summed + tap_rows[tap] * conv_grad[here + tap : here + tap + rows, :]
+                )
                 start = 8 + here - tap
                 tap_sums[tap] = tap_sums[tap] + jnp.sum(
                     grads * wide_feat[start : start + rows, :], axis=0, keepdims=True
                 )
-            outbox[chunk, block] = summed.astype(jnp.bfloat16)
-        filler = [jnp.zeros((per_chunk - taps_count, width), jnp.float32)]
-        shares[dp_rank, chunk, :, seq_len : seq_len + width] = jnp.concatenate(
-            tap_sums + (filler if per_chunk > taps_count else []), axis=0
-        )
+            put(block, summed.astype(jnp.bfloat16))
+        if per_chunk > taps_count:
+            tap_sums.append(jnp.zeros((per_chunk - taps_count, width), jnp.float32))
+        return jnp.concatenate(tap_sums, axis=0)
+
+    edge_zero = jnp.zeros((8, width), jnp.float32)
+
+    def put_out(chunk):
+        def put(block, value):
+            outbox[chunk, block] = value
+
+        return put
+
+    def keep_shares(chunk, lags, tap_share):
+        for lag in range(blocks):
+            shares[dp_rank, chunk, :, lag * rows : (lag + 1) * rows] = lags[lag]
+        shares[dp_rank, chunk, :, seq_len : seq_len + width] = tap_share
+
+    def send_shares(chunk):
+        for step in range(1, dp_count):
+            send(
+                shares.at[dp_rank, chunk],
+                shares.at[dp_rank, chunk],
+                send_share,
+                recv_share,
+                {"dp": lax.rem(dp_rank + step, dp_count)},
+            )
+
+    def own_columns(chunk):
+        return feature_out.at[:, columns(me, chunk)]
+
+    def do_early(chunk, carry):
+        landed = inbox.at[chunk, 0 : blocks + half]
+        pltpu.make_async_copy(landed, landed, recv_in.at[chunk]).wait()
+        tap_rows = tap_rows_of(me, chunk)
+        wide_feat[0:8, :] = edge_zero
+        lags = convolve(
+            tap_rows,
+            lambda block: inbox[chunk, blocks + block],
+            lambda block: inbox[chunk, block],
+            lambda index: filters[pl.ds(chunk * per_chunk + index, 1), :],
+            half,
+            blocks,
+        )
+        bundle = late_landed.at[chunk]
+        pltpu.make_async_copy(bundle, bundle, recv_landed.at[chunk]).wait()
+        lent = half * rows
+        conv_grad[lent : lent + 8, :] = late_landed[chunk, :, lent + width : lent + 2 * width]
+        tap_share = finish(tap_rows, half, put_out(chunk))
+        tap_share = tap_share + late_landed[chunk, :, lent : lent + width]
+        for lag in range(half):
+            lags[lag] = lags[lag] + late_landed[chunk, :, lag * rows : (lag + 1) * rows]
+        keep_shares(chunk, lags, tap_share)
+        other = half - 1 - me
+        send(outbox.at[chunk, other], own_columns(chunk), send_out, recv_out, {"ctx": other})
+        pltpu.make_async_copy(outbox.at[chunk, me], own_columns(chunk), recv_out).start()
+        send_shares(chunk)
+        return carry
+
+    def do_late(chunk, carry):
+        owner = me - half
+        landed = late_inbox.at[chunk]
+        pltpu.make_async_copy(landed, landed, recv_late.at[chunk]).wait()
+        edge = late_edge.at[chunk]
+        pltpu.make_async_copy(edge, edge, recv_edge.at[chunk]).wait()
+        lent_here = lent_filters.at[chunk]
+        pltpu.make_async_copy(lent_here, lent_here, recv_lent.at[chunk]).wait()
+        tap_rows = tap_rows_of(owner, chunk)
+        wide_feat[0:8, :] = late_edge[chunk].astype(jnp.float32)[8:16]
+        lags = convolve(
+            tap_rows,
+            lambda block: late_inbox[chunk, half + block],
+            lambda block: late_inbox[chunk, block],
+            lambda index: lent_filters[chunk, pl.ds(index, 1), :],
+            half,
+            half,
+        )
+        conv_grad[half * rows : half * rows + 8, :] = edge_zero
+
+        def put(block, value):
+            late_outbox[chunk, block] = value
+
+        tap_share = finish(tap_rows, half, put)
+        lent = half * rows
+        for lag in range(half):
+            late_share[chunk, :, lag * rows : (lag + 1) * rows] = lags[lag]
+        late_share[chunk, :, lent : lent + width] = tap_share
+        late_share[chunk, :, lent + width : lent + 2 * width] = conv_grad[0:8, :]
+        send(
+            late_share.at[chunk],
+            late_landed.at[chunk],
+            send_late,
+            recv_landed.at[chunk],
+            {"ctx": owner},
+        )
+        place = feature_out.at[:, columns(owner, chunk)]
+        other = half - 1 - owner
+        send(late_outbox.at[chunk, other], place, send_out, recv_out, {"ctx": half + other})
+        pltpu.make_async_copy(late_outbox.at[chunk, owner], place, recv_out).start()
+
+        landed = inbox.at[chunk]
+        pltpu.make_async_copy(landed, landed, recv_in.at[chunk]).wait()
+        tap_rows = tap_rows_of(me, chunk)
+        wide_feat[0:8, :] = edge_zero
+        lags = convolve(
+            tap_rows,
+            lambda block: inbox[chunk, blocks + block],
+            lambda block: inbox[chunk, block],
+            lambda index: filters[pl.ds(chunk * per_chunk + index, 1), :],
+            blocks,
+            blocks,
+        )
+        conv_grad[seq_len : seq_len + 8, :] = edge_zero
+        tap_share = finish(tap_rows, blocks, put_out(chunk))
+        keep_shares(chunk, lags, tap_share)
         for step in range(1, blocks):
             target = lax.rem(me + step, blocks)
-            pltpu.make_async_remote_copy(
-                src_ref=outbox.at[chunk, target],
-                dst_ref=feature_out.at[:, columns(me, chunk)],
-                send_sem=send_out,
-                recv_sem=recv_out,
-                device_id={"ctx": target},
-                device_id_type=MESH,
-            ).start()
-        pltpu.make_async_copy(
-            outbox.at[chunk, me], feature_out.at[:, columns(me, chunk)], recv_out
-        ).start()
-        for step in range(1, dp_count):
-            pltpu.make_async_remote_copy(
-                src_ref=shares.at[dp_rank, chunk],
-                dst_ref=shares.at[dp_rank, chunk],
-                send_sem=send_share,
-                recv_sem=recv_share,
-                device_id={"dp": lax.rem(dp_rank + step, dp_count)},
-                device_id_type=MESH,
-            ).start()
+            send(
+                outbox.at[chunk, target], own_columns(chunk), send_out, recv_out, {"ctx": target}
+            )
+        pltpu.make_async_copy(outbox.at[chunk, me], own_columns(chunk), recv_out).start()
+        send_shares(chunk)
         return carry
 
-    lax.fori_loop(0, chunks, do_chunk, 0)
-
-    others = shares.at[0 : dp_count - 1]
-    pltpu.make_async_copy(others, others, recv_share).wait()
-    pltpu.make_async_copy(others, others, send_share).wait()
+    def drain(ref, sem):
+        pltpu.make_async_copy(ref, ref, sem).wait()
+
+    @pl.when(is_early)
+    def _():
+        lax.fori_loop(0, chunks, do_early, 0)
+
+    @pl.when(is_late)
+    def _():
+        lax.fori_loop(0, chunks, do_late, 0)
+
+    drain(shares.at[0 : dp_count - 1], recv_share)
     filter_scale = 1.0 / math.sqrt(dp_count * group * seq_len)
     tap_scale = 1.0 / math.sqrt(dp_count * seq_len)
     for chunk in range(chunks):
@@ -446,14 +639,27 @@
         filter_out[chunk * per_chunk : (chunk + 1) * per_chunk, :] = (
             total[:, :seq_len] * filter_scale
         )
-        tap_out[:, chunk * width : (chunk + 1) * width] = (
-            total[:taps_count, seq_len:] * tap_scale
-        )
-    inputs_sent = inbox.at[:, 0 : 2 * blocks - 1]
-    pltpu.make_async_copy(inputs_sent, inputs_sent, send_in).wait()
-    outputs_sent = outbox.at[:, 0 : blocks - 1]
-    pltpu.make_async_copy(outputs_sent, outputs_sent, send_out).wait()
-    pltpu.make_async_copy(outbox, outbox, recv_out).wait()
+        tap_out[:, chunk * width : (chunk + 1) * width] = total[:taps_count, seq_len:] * tap_scale
+    drain(shares.at[0 : dp_count - 1], send_share)
+
+    @pl.when(is_early)
+    def _():
+        drain(lent_filters, send_lent)
+        drain(inbox.at[:, 0 : 2 * blocks - 1], send_in)
+        drain(outbox.at[:, 0 : half - 1], send_out)
+
+    @pl.when(me == half - 1)
+    def _():
+        for _ in range(half):
+            drain(late_edge, send_edge)
+
+    @pl.when(is_late)
+    def _():
+        drain(inbox, send_in)
+        drain(outbox, send_out)
+        drain(late_share, send_late)
+
+    drain(outbox, recv_out)
 
 
 def fused_body(arriving, features, short_taps, filters):
@@ -466,11 +672,15 @@
     group = own_width // filter_count
     taps_count = short_taps.shape[1]
     width = rows
+    half = blocks // 2
     chunks = own_width // width
     per_chunk = width // group
+    lent = half * rows
     sizes = (blocks, dp_count, pipe_count, chunks, rows, width, group, taps_count)
-    anywhere = pl.BlockSpec(memory_space=pl.ANY)
+    anywhere = pl.BlockSpec(memory_space=pltpu.HBM)
     vmem = pl.BlockSpec(memory_space=pltpu.VMEM)
+    one_sem = pltpu.SemaphoreType.DMA
+    chunk_sems = pltpu.SemaphoreType.DMA((chunks,))
     feature_grads, filter_grads, tap_grads = pl.pallas_call(
         functools.partial(fused_kernel, sizes),
         out_shape=(
@@ -478,29 +688,50 @@
             jax.ShapeDtypeStruct((filter_count, seq_len), jnp.float32),
             jax.ShapeDtypeStruct((taps_count, own_width), jnp.float32),
         ),
-        in_specs=[anywhere, anywhere, vmem, vmem],
+        in_specs=[anywhere] * 4,
         out_specs=(anywhere, vmem, vmem),
         scratch_shapes=[
+            pltpu.VMEM((taps_count, channels // width, width), jnp.float32),
+            pltpu.VMEM((filter_count, seq_len), jnp.float32),
+            pltpu.VMEM((chunks, per_chunk, lent), jnp.float32),
             pltpu.VMEM((chunks, 2 * blocks, rows, width), jnp.bfloat16),
+            pltpu.VMEM((chunks, 2 * half, rows, width), jnp.bfloat16),
+            pltpu.VMEM((chunks, 16, width), jnp.bfloat16),
             pltpu.VMEM((chunks, blocks, rows, width), jnp.bfloat16),
+            pltpu.VMEM((chunks, half, rows, width), jnp.bfloat16),
             pltpu.VMEM((dp_count, chunks, per_chunk, seq_len + width), jnp.float32),
+            pltpu.VMEM((chunks, per_chunk, lent + 2 * width), jnp.float32),
+            pltpu.VMEM((chunks, per_chunk, lent + 2 * width), jnp.float32),
             pltpu.VMEM((seq_len + 8, width), jnp.float32),
             pltpu.VMEM((seq_len, 2 * width), jnp.bfloat16),
             pltpu.VMEM((seq_len, 2 * width), jnp.bfloat16),
             pltpu.VMEM((seq_len, 2 * width), jnp.bfloat16),
             pltpu.VMEM((seq_len + 8, width), jnp.float32),
             pltpu.VMEM((blocks * per_chunk * 8, width), jnp.float32),
-            pltpu.SemaphoreType.DMA,
-            pltpu.SemaphoreType.DMA((chunks,)),
-            pltpu.SemaphoreType.DMA,
-            pltpu.SemaphoreType.DMA,
-            pltpu.SemaphoreType.DMA,
-            pltpu.SemaphoreType.DMA,
+            pltpu.SemaphoreType.DMA((2,)),
+            one_sem,
+            chunk_sems,
+            chunk_sems,
+            one_sem,
+            chunk_sems,
+            one_sem,
+            chunk_sems,
+            one_sem,
+            chunk_sems,
+            one_sem,
+            one_sem,
+            one_sem,
+            one_sem,
         ],
         compiler_params=pltpu.CompilerParams(
-            collective_id=0, has_side_effects=True, vmem_limit_bytes=32 * 1024 * 1024
+            collective_id=0, has_side_effects=True, vmem_limit_bytes=60 * 1024 * 1024
         ),
-    )(arriving[0, 0], features[0, 0], short_taps[0], filters[0])
+    )(
+        arriving[0, 0],
+        features[0, 0],
+        short_taps.reshape(taps_count, channels // width, width),
+        filters,
+    )
     return (feature_grads[None, None], filter_grads[None], tap_grads[None])
 
 
@@ -511,8 +742,7 @@
     group = own_width // own_filters
     return (
         rows == 128
-        and blocks % 2 == 0
-        and blocks <= 8
+        and blocks == 4
         and mesh.shape["pipe"] == 2
         and own_width % rows == 0
         and rows % group == 0

time: 80.8 us -> 91.4 us (1.13)
  Pallas kernels: 74.2 us -> 86.2 us
  local copies, waits for them, and re-layouts: 5.72 us -> 4.38 us
    pallas_call x1, Pallas kernels: 74.2 us -> 86.2 us  [fused_body(): pl.pallas_call(functools.partial(fused_kernel, sizes), out_shape=(jax.Sha...]
    unnamed x10 -> x5, local copies, waits for them, and re-layouts: 5.72 us -> 4.38 us
where the time goes in v2:
time: 91.4 us; the launch traced here: 91.2 us
  Pallas kernels  86.2 us (94%)
  local copies, waits for them, and re-layouts  4.38 us (5%)
    pallas_call x1, Pallas kernels, fused_body(): pl.pallas_call(functools.partial(fused_kernel, sizes), out_shape=(jax.Sha...  86.2 us
    unnamed x5, local copies, waits for them, and re-layouts  4.38 us

profile of v2, /device:TPU:0, one launch (start us, length us, event | category | flops | bytes accessed | tf_op | source)
XLA Modules:
  0.0 91.2 jit_solution(11631027345026032535)
XLA Ops:
  0.6 86.2 %shard_map.67 = (bf16[128,4096]{1,0:T(8,128)(2,1)}, f32[64,512]{1,0:T(8,128)}, f32[7,1024]{1,0:T(8,128)}) custom-call(bf16[128,4096]{1,0:T(8,128)(2,1)} %bitcast.6, bf16[128,4096]{1,0:T(8,128)(2,1)} %bitcast.7, f32[7,32,128]{2,1,0:T(8,128)} %bitcast.10, f32[1,64,512]{2,1,0:T(8,128)} %filters_all.1), custom_call_target="tpu_custom_call" | custom-call | tf_op jit(solution)/shard_map/pallas_call | solution.py:684
  86.8 1.4 %copy.7 = f32[1,7,1024]{2,0,1:T(1,128)} copy(f32[1,7,1024]{2,1,0:T(8,128)} %bitcast.11) | data formatting | bytes 57344
  88.2 0.0 copy-start
  88.2 2.3 %copy.10 = bf16[1,1,128,4096]{3,2,1,0:T(8,128)(2,1)} copy(bf16[1,1,128,4096]{3,2,1,0:T(8,128)(2,1)} %bitcast.8) | data formatting | bytes 2097152
  90.6 0.0 copy-done
  90.6 0.7 copy.11
Async XLA Ops:
  88.2 2.3 %copy-start = (f32[64,512]{1,0:T(8,128)S(1)}, f32[64,512]{1,0:T(8,128)}, u32[]{:S(2)}) copy-start(f32[64,512]{1,0:T(8,128)} %get-tuple-element.7) | copy-start | bytes 393220

commit v3 on v2

--- a/solution.py
+++ b/solution.py
@@ -214,8 +214,9 @@
     late_landed,
     wide_feat,
     split_in,
-    pair_grad,
-    twin_grad,
+    grad_cols,
+    turned,
+    conv_cols,
     conv_grad,
     diagonals,
     local_sems,
@@ -373,10 +374,11 @@
     row_index = lax.broadcasted_iota(jnp.int32, (rows, rows), 0)
     lane_index = lax.broadcasted_iota(jnp.int32, (rows, rows), 1)
     upper = lane_index >= row_index
-    lane_group = lane_index // group
+    lower = row_index >= lane_index
+    mirror = (lax.rem(row_index + lane_index, rows) == 0).astype(jnp.bfloat16)
     zero_tile = jnp.zeros((rows, rows), jnp.float32)
 
-    def convolve(tap_rows, feat_at, grad_at, kernel_at, feat_blocks, grad_blocks):
+    def convolve(tap_rows, feat_at, grad_at, kernel_rows, feat_blocks, grad_blocks):
         for block in range(feat_blocks):
             wide_feat[8 + block * rows : 8 + (block + 1) * rows, :] = feat_at(block).astype(
                 jnp.float32
@@ -387,25 +389,27 @@
             for tap in range(taps_count):
                 start = 8 + block * rows - tap
                 summed = summed + tap_rows[tap] * wide_feat[start : start + rows, :]
+            summed = summed.T
             high = summed.astype(jnp.bfloat16)
-            low = (summed - high.astype(jnp.float32)).astype(jnp.bfloat16)
-            split_in[here, 0:width] = high
-            split_in[here, width : 2 * width] = low
+            split_in[0, :, here] = high
+            split_in[1, :, here] = (summed - high.astype(jnp.float32)).astype(jnp.bfloat16)
+        for block in range(grad_blocks):
+            grad_cols[:, block * rows : (block + 1) * rows] = grad_at(block).T
+        grad_cols[:, grad_blocks * rows : (grad_blocks + feat_blocks - 1) * rows] = jnp.zeros(
+            (width, (feat_blocks - 1) * rows), jnp.bfloat16
+        )
         for block in range(grad_blocks):
             here = slice(block * rows, (block + 1) * rows)
-            grad = grad_at(block)
-            twin_grad[here, 0:width] = grad
-            twin_grad[here, width : 2 * width] = grad
-            pair_grad[here, 0:width] = grad
-            if block:
-                pair_grad[(block - 1) * rows : block * rows, width : 2 * width] = grad
-        pair_grad[(grad_blocks - 1) * rows : grad_blocks * rows, width : 2 * width] = jnp.zeros(
-            (rows, width), jnp.bfloat16
-        )
-
-        def do_filter(index, inner):
-            ours = lane_group == index
-            kernel_row = kernel_at(index)
+            whole = kernel_rows[:, here]
+            high = whole.astype(jnp.bfloat16)
+            low = (whole - high.astype(jnp.float32)).astype(jnp.bfloat16)
+            turned[:, here] = jnp.dot(
+                high, mirror, preferred_element_type=jnp.float32
+            ) + jnp.dot(low, mirror, preferred_element_type=jnp.float32)
+
+        def one_filter(index):
+            ours = pl.ds(pl.multiple_of(index * group, group), group)
+            kernel_row = turned[pl.ds(index, 1), :]
             highs, lows = [], []
             last = zero_tile
             for block in range(grad_blocks):
@@ -413,63 +417,68 @@
                     kernel_row[:, block * rows : (block + 1) * rows], (rows, rows)
                 )
                 rolled = pltpu.roll(spread, 0, 1, stride=1, stride_axis=0)
-                tile = jnp.where(upper, rolled, last)
+                tile = jnp.where(lower, rolled, last)
                 last = rolled
                 high = tile.astype(jnp.bfloat16)
                 highs.append(high)
                 lows.append((tile - high.astype(jnp.float32)).astype(jnp.bfloat16))
             table = jnp.concatenate(
-                [jnp.concatenate(highs, axis=1), jnp.concatenate(lows, axis=1)], axis=0
-            )
-            for block in range(0, feat_blocks, 2):
-                product = jnp.dot(
-                    table[:, : (grad_blocks - block) * rows],
-                    pair_grad[block * rows : grad_blocks * rows, :],
-                    preferred_element_type=jnp.float32,
+                [jnp.concatenate(highs, axis=0), jnp.concatenate(lows, axis=0)], axis=1
+            )
+            shifted = jnp.concatenate(
+                [
+                    grad_cols[ours, block * rows : (block + grad_blocks) * rows]
+                    for block in range(feat_blocks)
+                ],
+                axis=0,
+            )
+            product = jnp.dot(shifted, table, preferred_element_type=jnp.float32)
+            both = product[:, :rows] + product[:, rows:]
+            for block in range(feat_blocks):
+                conv_cols[ours, block * rows : (block + 1) * rows] = both[
+                    block * group : (block + 1) * group
+                ]
+            picked = jnp.concatenate(
+                [
+                    split_in[part, ours, block * rows : (block + 1) * rows]
+                    for part in range(2)
+                    for block in range(feat_blocks)
+                ],
+                axis=0,
+            )
+            sums = jnp.dot(
+                picked.T,
+                jnp.concatenate([shifted, shifted], axis=0),
+                preferred_element_type=jnp.float32,
+            )
+            for lag in range(grad_blocks):
+                following = (
+                    sums[:, (lag + 1) * rows : (lag + 2) * rows]
+                    if lag + 1 < grad_blocks
+                    else zero_tile
                 )
-                both = product[:rows] + product[rows:]
-                for side in range(2):
-                    here = slice((block + side) * rows, (block + side + 1) * rows)
-                    conv_grad[here, :] = jnp.where(
-                        ours, both[:, side * width : (side + 1) * width], conv_grad[here, :]
+                merged = jnp.where(upper, sums[:, lag * rows : (lag + 1) * rows], following)
+                folded = [merged[0:8]]
+                for part in range(1, rows // 8):
+                    folded.append(
+                        pltpu.roll(merged[part * 8 : part * 8 + 8], rows - part * 8, 1)
                     )
-            ours_twice = jnp.concatenate([ours, ours], axis=1)
-            picked = [
-                jnp.where(
-                    ours_twice,
-                    split_in[block * rows : (block + 1) * rows, :],
-                    jnp.zeros((rows, 2 * width), jnp.bfloat16),
-                )
-                for block in range(feat_blocks)
-            ]
-            sums = [None] * grad_blocks
-            for block in range(0, grad_blocks, 2):
-                product = lax.dot_general(
-                    jnp.concatenate(picked[: block + 2], axis=0),
-                    twin_grad[block * rows : (block + 2) * rows, :],
-                    (((1,), (1,)), ((), ())),
-                    preferred_element_type=jnp.float32,
-                )
-                for side in range(2):
-                    for early in range(min(feat_blocks, block + side + 1)):
-                        lag = block + side - early
-                        piece = product[
-                            early * rows : (early + 1) * rows, side * rows : (side + 1) * rows
-                        ]
-                        sums[lag] = piece if sums[lag] is None else sums[lag] + piece
-            for lag in range(grad_blocks):
-                following = sums[lag + 1] if lag + 1 < grad_blocks else zero_tile
-                merged = jnp.where(upper, sums[lag], following)
-                folded = merged[0:8]
-                for part in range(1, rows // 8):
-                    folded = folded + pltpu.roll(
-                        merged[part * 8 : part * 8 + 8], rows - part * 8, 1
-                    )
+                while len(folded) > 1:
+                    folded = [
+                        folded[place] + folded[place + 1] for place in range(0, len(folded), 2)
+                    ]
                 place = pl.multiple_of((lag * per_chunk + index) * 8, 8)
-                diagonals[pl.ds(place, 8), :] = folded
+                diagonals[pl.ds(place, 8), :] = folded[0]
+
+        def do_filters(index, inner):
+            one_filter(2 * index)
+            one_filter(2 * index + 1)
             return inner
 
-        lax.fori_loop(0, per_chunk, do_filter, 0)
+        lax.fori_loop(0, per_chunk // 2, do_filters, 0)
+        for block in range(feat_blocks):
+            here = slice(block * rows, (block + 1) * rows)
+            conv_grad[here, :] = conv_cols[:, here].T
         count = grad_blocks * per_chunk
         lagged = diagonals[pl.ds(0, count, stride=8), :]
         for turn in range(1, 8):
@@ -534,7 +543,7 @@
             tap_rows,
             lambda block: inbox[chunk, blocks + block],
             lambda block: inbox[chunk, block],
-            lambda index: filters[pl.ds(chunk * per_chunk + index, 1), :],
+            filters[pl.ds(pl.multiple_of(chunk * per_chunk, 8), per_chunk), :],
             half,
             blocks,
         )
@@ -567,7 +576,7 @@
             tap_rows,
             lambda block: late_inbox[chunk, half + block],
             lambda block: late_inbox[chunk, block],
-            lambda index: lent_filters[chunk, pl.ds(index, 1), :],
+            lent_filters[chunk],
             half,
             half,
         )
@@ -602,7 +611,7 @@
             tap_rows,
             lambda block: inbox[chunk, blocks + block],
             lambda block: inbox[chunk, block],
-            lambda index: filters[pl.ds(chunk * per_chunk + index, 1), :],
+            filters[pl.ds(pl.multiple_of(chunk * per_chunk, 8), per_chunk), :],
             blocks,
             blocks,
         )
@@ -703,9 +712,10 @@
             pltpu.VMEM((chunks, per_chunk, lent + 2 * width), jnp.float32),
             pltpu.VMEM((chunks, per_chunk, lent + 2 * width), jnp.float32),
             pltpu.VMEM((seq_len + 8, width), jnp.float32),
-            pltpu.VMEM((seq_len, 2 * width), jnp.bfloat16),
-            pltpu.VMEM((seq_len, 2 * width), jnp.bfloat16),
-            pltpu.VMEM((seq_len, 2 * width), jnp.bfloat16),
+            pltpu.VMEM((2, width, seq_len), jnp.bfloat16),
+            pltpu.VMEM((width, 2 * seq_len), jnp.bfloat16),
+            pltpu.VMEM((per_chunk, seq_len), jnp.float32),
+            pltpu.VMEM((width, seq_len), jnp.float32),
             pltpu.VMEM((seq_len + 8, width), jnp.float32),
             pltpu.VMEM((blocks * per_chunk * 8, width), jnp.float32),
             pltpu.SemaphoreType.DMA((2,)),

time: 91.4 us -> 77.2 us (0.84)
  Pallas kernels: 86.2 us -> 71.9 us
    pallas_call x1, Pallas kernels: 86.2 us -> 71.9 us  [fused_body(): pl.pallas_call(functools.partial(fused_kernel, sizes), out_shape=(jax.Sha...]
where the time goes in v3:
time: 77.2 us; the launch traced here: 77 us
  Pallas kernels  71.9 us (93%)
  local copies, waits for them, and re-layouts  4.38 us (6%)
    pallas_call x1, Pallas kernels, fused_body(): pl.pallas_call(functools.partial(fused_kernel, sizes), out_shape=(jax.Sha...  71.9 us
    unnamed x5, local copies, waits for them, and re-layouts  4.38 us

profile of v3, /device:TPU:0, one launch (start us, length us, event | category | flops | bytes accessed | tf_op | source)
XLA Modules:
  0.0 77.0 jit_solution(5812364775700526163)
XLA Ops:
  0.6 71.9 %shard_map.67 = (bf16[128,4096]{1,0:T(8,128)(2,1)}, f32[64,512]{1,0:T(8,128)}, f32[7,1024]{1,0:T(8,128)}) custom-call(bf16[128,4096]{1,0:T(8,128)(2,1)} %bitcast.6, bf16[128,4096]{1,0:T(8,128)(2,1)} %bitcast.7, f32[7,32,128]{2,1,0:T(8,128)} %bitcast.10, f32[1,64,512]{2,1,0:T(8,128)} %filters_all.1), custom_call_target="tpu_custom_call" | custom-call | tf_op jit(solution)/shard_map/pallas_call | solution.py:693
  72.6 1.4 %copy.7 = f32[1,7,1024]{2,0,1:T(1,128)} copy(f32[1,7,1024]{2,1,0:T(8,128)} %bitcast.11) | data formatting | bytes 57344
  74.0 0.0 copy-start
  74.0 2.3 %copy.10 = bf16[1,1,128,4096]{3,2,1,0:T(8,128)(2,1)} copy(bf16[1,1,128,4096]{3,2,1,0:T(8,128)(2,1)} %bitcast.8) | data formatting | bytes 2097152
  76.3 0.0 copy-done
  76.3 0.7 copy.11
Async XLA Ops:
  74.0 2.3 %copy-start = (f32[64,512]{1,0:T(8,128)S(1)}, f32[64,512]{1,0:T(8,128)}, u32[]{:S(2)}) copy-start(f32[64,512]{1,0:T(8,128)} %get-tuple-element.7) | copy-start | bytes 393220

commit v4 on v3

--- a/solution.py
+++ b/solution.py
@@ -377,6 +377,8 @@
     lower = row_index >= lane_index
     mirror = (lax.rem(row_index + lane_index, rows) == 0).astype(jnp.bfloat16)
     zero_tile = jnp.zeros((rows, rows), jnp.float32)
+    edge_zero = jnp.zeros((8, width), jnp.float32)
+    zero_strip = jnp.zeros((16, rows), jnp.bfloat16)
 
     def convolve(tap_rows, feat_at, grad_at, kernel_rows, feat_blocks, grad_blocks):
         for block in range(feat_blocks):
@@ -411,17 +413,26 @@
             ours = pl.ds(pl.multiple_of(index * group, group), group)
             kernel_row = turned[pl.ds(index, 1), :]
             highs, lows = [], []
-            last = zero_tile
+            last = [(zero_strip, zero_strip)] * (rows // 16)
             for block in range(grad_blocks):
                 spread = jnp.broadcast_to(
-                    kernel_row[:, block * rows : (block + 1) * rows], (rows, rows)
+                    kernel_row[:, block * rows : (block + 1) * rows], (16, rows)
                 )
-                rolled = pltpu.roll(spread, 0, 1, stride=1, stride_axis=0)
-                tile = jnp.where(lower, rolled, last)
-                last = rolled
-                high = tile.astype(jnp.bfloat16)
-                highs.append(high)
-                lows.append((tile - high.astype(jnp.float32)).astype(jnp.bfloat16))
+                base = pltpu.roll(spread, 0, 1, stride=1, stride_axis=0)
+                high = base.astype(jnp.bfloat16)
+                low = (base - high.astype(jnp.float32)).astype(jnp.bfloat16)
+                strips = [
+                    (
+                        pltpu.roll(high, part * 16, 1) if part else high,
+                        pltpu.roll(low, part * 16, 1) if part else low,
+                    )
+                    for part in range(rows // 16)
+                ]
+                for part in range(rows // 16):
+                    keep = lower[part * 16 : part * 16 + 16]
+                    highs.append(jnp.where(keep, strips[part][0], last[part][0]))
+                    lows.append(jnp.where(keep, strips[part][1], last[part][1]))
+                last = strips
             table = jnp.concatenate(
                 [jnp.concatenate(highs, axis=0), jnp.concatenate(lows, axis=0)], axis=1
             )
@@ -490,25 +501,24 @@
         ]
 
     def finish(tap_rows, feat_blocks, put):
-        tap_sums = [jnp.zeros((1, width), jnp.float32)] * taps_count
+        tap_sums = [edge_zero] * taps_count
         for block in range(feat_blocks):
             here = block * rows
             summed = zero_tile
-            grads = conv_grad[here : here + rows, :]
+            feats = wide_feat[8 + here : 8 + here + rows, :]
             for tap in range(taps_count):
-                summed = (
-                    summed + tap_rows[tap] * conv_grad[here + tap : here + tap + rows, :]
-                )
-                start = 8 + here - tap
+                grads = conv_grad[here + tap : here + tap + rows, :]
+                summed = summed + tap_rows[tap] * grads
+                pairs = grads * feats
                 tap_sums[tap] = tap_sums[tap] + jnp.sum(
-                    grads * wide_feat[start : start + rows, :], axis=0, keepdims=True
+                    pairs.reshape(rows // 8, 8, width), axis=0
                 )
             put(block, summed.astype(jnp.bfloat16))
+        tap_sums = [jnp.sum(value, axis=0, keepdims=True) for value in tap_sums]
         if per_chunk > taps_count:
             tap_sums.append(jnp.zeros((per_chunk - taps_count, width), jnp.float32))
         return jnp.concatenate(tap_sums, axis=0)
 
-    edge_zero = jnp.zeros((8, width), jnp.float32)
 
     def put_out(chunk):
         def put(block, value):

time: 77.2 us -> 79.8 us (1.034)
  Pallas kernels: 71.9 us -> 74.6 us
    pallas_call x1, Pallas kernels: 71.9 us -> 74.6 us  [fused_body(): pl.pallas_call(functools.partial(fused_kernel, sizes), out_shape=(jax.Sha...]
where the time goes in v4:
time: 79.8 us; the launch traced here: 79.6 us
  Pallas kernels  74.6 us (93%)
  local copies, waits for them, and re-layouts  4.38 us (5%)
    pallas_call x1, Pallas kernels, fused_body(): pl.pallas_call(functools.partial(fused_kernel, sizes), out_shape=(jax.Sha...  74.6 us
    unnamed x5, local copies, waits for them, and re-layouts  4.38 us

profile of v4, /device:TPU:0, one launch (start us, length us, event | category | flops | bytes accessed | tf_op | source)
XLA Modules:
  0.0 79.6 jit_solution(16686517106319710762)
XLA Ops:
  0.6 74.6 %shard_map.67 = (bf16[128,4096]{1,0:T(8,128)(2,1)}, f32[64,512]{1,0:T(8,128)}, f32[7,1024]{1,0:T(8,128)}) custom-call(bf16[128,4096]{1,0:T(8,128)(2,1)} %bitcast.6, bf16[128,4096]{1,0:T(8,128)(2,1)} %bitcast.7, f32[7,32,128]{2,1,0:T(8,128)} %bitcast.10, f32[1,64,512]{2,1,0:T(8,128)} %filters_all.1), custom_call_target="tpu_custom_call" | custom-call | tf_op jit(solution)/shard_map/pallas_call | solution.py:703
  75.2 1.4 %copy.7 = f32[1,7,1024]{2,0,1:T(1,128)} copy(f32[1,7,1024]{2,1,0:T(8,128)} %bitcast.11) | data formatting | bytes 57344
  76.6 0.0 copy-start
  76.6 2.3 %copy.10 = bf16[1,1,128,4096]{3,2,1,0:T(8,128)(2,1)} copy(bf16[1,1,128,4096]{3,2,1,0:T(8,128)(2,1)} %bitcast.8) | data formatting | bytes 2097152
  78.9 0.0 copy-done
  78.9 0.7 copy.11
Async XLA Ops:
  76.6 2.3 %copy-start = (f32[64,512]{1,0:T(8,128)S(1)}, f32[64,512]{1,0:T(8,128)}, u32[]{:S(2)}) copy-start(f32[64,512]{1,0:T(8,128)} %get-tuple-element.7) | copy-start | bytes 393220

commit v5 on v3

--- a/solution.py
+++ b/solution.py
@@ -234,7 +234,7 @@
     send_share,
     recv_share,
 ):
-    blocks, dp_count, pipe_count, chunks, rows, width, group, taps_count = sizes
+    blocks, dp_count, pipe_count, chunks, halved, rows, width, group, taps_count = sizes
     seq_len = blocks * rows
     half = blocks // 2
     own_width = chunks * width
@@ -293,7 +293,9 @@
         ).start()
 
     def send_chunk(chunk, carry):
-        @pl.when(is_early)
+        is_halved = chunk < halved
+
+        @pl.when(jnp.logical_and(is_early, is_halved))
         def _():
             send(
                 filters_all.at[0, pl.ds(pl.multiple_of(chunk * per_chunk, 8), per_chunk), 0 : half * rows],
@@ -303,7 +305,7 @@
                 {"ctx": me + half},
             )
 
-        @pl.when(me == half - 1)
+        @pl.when(jnp.logical_and(me == half - 1, is_halved))
         def _():
             for owner in range(half):
                 send(
@@ -314,7 +316,7 @@
                     {"ctx": half + owner},
                 )
 
-        @pl.when(is_late)
+        @pl.when(jnp.logical_and(is_late, is_halved))
         def _():
             for step in range(half):
                 owner = lax.rem(me + step, half)
@@ -352,7 +354,11 @@
             )
             if step:
 
-                @pl.when(jnp.logical_or(is_early, target >= half))
+                @pl.when(
+                    jnp.logical_or(
+                        jnp.logical_or(is_early, target >= half), jnp.logical_not(is_halved)
+                    )
+                )
                 def _():
                     send(
                         features.at[:, columns(target, chunk)],
@@ -377,6 +383,7 @@
     lower = row_index >= lane_index
     mirror = (lax.rem(row_index + lane_index, rows) == 0).astype(jnp.bfloat16)
     zero_tile = jnp.zeros((rows, rows), jnp.float32)
+    edge_zero = jnp.zeros((8, width), jnp.float32)
 
     def convolve(tap_rows, feat_at, grad_at, kernel_rows, feat_blocks, grad_blocks):
         for block in range(feat_blocks):
@@ -490,25 +497,24 @@
         ]
 
     def finish(tap_rows, feat_blocks, put):
-        tap_sums = [jnp.zeros((1, width), jnp.float32)] * taps_count
+        tap_sums = [edge_zero] * taps_count
         for block in range(feat_blocks):
             here = block * rows
             summed = zero_tile
-            grads = conv_grad[here : here + rows, :]
+            feats = wide_feat[8 + here : 8 + here + rows, :]
             for tap in range(taps_count):
-                summed = (
-                    summed + tap_rows[tap] * conv_grad[here + tap : here + tap + rows, :]
-                )
-                start = 8 + here - tap
+                grads = conv_grad[here + tap : here + tap + rows, :]
+                summed = summed + tap_rows[tap] * grads
+                pairs = grads * feats
                 tap_sums[tap] = tap_sums[tap] + jnp.sum(
-                    grads * wide_feat[start : start + rows, :], axis=0, keepdims=True
+                    pairs.reshape(rows // 8, 8, width), axis=0
                 )
             put(block, summed.astype(jnp.bfloat16))
+        tap_sums = [jnp.sum(value, axis=0, keepdims=True) for value in tap_sums]
         if per_chunk > taps_count:
             tap_sums.append(jnp.zeros((per_chunk - taps_count, width), jnp.float32))
         return jnp.concatenate(tap_sums, axis=0)
 
-    edge_zero = jnp.zeros((8, width), jnp.float32)
 
     def put_out(chunk):
         def put(block, value):
@@ -534,7 +540,7 @@
     def own_columns(chunk):
         return feature_out.at[:, columns(me, chunk)]
 
-    def do_early(chunk, carry):
+    def do_early(chunk):
         landed = inbox.at[chunk, 0 : blocks + half]
         pltpu.make_async_copy(landed, landed, recv_in.at[chunk]).wait()
         tap_rows = tap_rows_of(me, chunk)
@@ -560,9 +566,8 @@
         send(outbox.at[chunk, other], own_columns(chunk), send_out, recv_out, {"ctx": other})
         pltpu.make_async_copy(outbox.at[chunk, me], own_columns(chunk), recv_out).start()
         send_shares(chunk)
-        return carry
-
-    def do_late(chunk, carry):
+
+    def do_late(chunk):
         owner = me - half
         landed = late_inbox.at[chunk]
         pltpu.make_async_copy(landed, landed, recv_late.at[chunk]).wait()
@@ -603,6 +608,7 @@
         send(late_outbox.at[chunk, other], place, send_out, recv_out, {"ctx": half + other})
         pltpu.make_async_copy(late_outbox.at[chunk, owner], place, recv_out).start()
 
+    def do_whole(chunk):
         landed = inbox.at[chunk]
         pltpu.make_async_copy(landed, landed, recv_in.at[chunk]).wait()
         tap_rows = tap_rows_of(me, chunk)
@@ -625,18 +631,28 @@
             )
         pltpu.make_async_copy(outbox.at[chunk, me], own_columns(chunk), recv_out).start()
         send_shares(chunk)
-        return carry
 
     def drain(ref, sem):
         pltpu.make_async_copy(ref, ref, sem).wait()
 
-    @pl.when(is_early)
-    def _():
-        lax.fori_loop(0, chunks, do_early, 0)
-
-    @pl.when(is_late)
-    def _():
-        lax.fori_loop(0, chunks, do_late, 0)
+    def do_chunk(chunk, carry):
+        is_halved = chunk < halved
+
+        @pl.when(jnp.logical_and(is_late, is_halved))
+        def _():
+            do_late(chunk)
+
+        @pl.when(jnp.logical_and(is_early, is_halved))
+        def _():
+            do_early(chunk)
+
+        @pl.when(jnp.logical_or(is_late, jnp.logical_not(is_halved)))
+        def _():
+            do_whole(chunk)
+
+        return carry
+
+    lax.fori_loop(0, chunks, do_chunk, 0)
 
     drain(shares.at[0 : dp_count - 1], recv_share)
     filter_scale = 1.0 / math.sqrt(dp_count * group * seq_len)
@@ -655,7 +671,8 @@
     def _():
         drain(lent_filters, send_lent)
         drain(inbox.at[:, 0 : 2 * blocks - 1], send_in)
-        drain(outbox.at[:, 0 : half - 1], send_out)
+        drain(outbox.at[0:halved, 0 : half - 1], send_out)
+        drain(outbox.at[halved:chunks, 0 : blocks - 1], send_out)
 
     @pl.when(me == half - 1)
     def _():
@@ -664,8 +681,10 @@
 
     @pl.when(is_late)
     def _():
-        drain(inbox, send_in)
-        drain(outbox, send_out)
+        drain(inbox.at[0:halved], send_in)
+        drain(inbox.at[halved:chunks, 0 : 2 * blocks - 1], send_in)
+        drain(outbox.at[:, 0 : blocks - 1], send_out)
+        drain(outbox.at[0:halved, 0 : half - 1], send_out)
         drain(late_share, send_late)
 
     drain(outbox, recv_out)
@@ -685,7 +704,8 @@
     chunks = own_width // width
     per_chunk = width // group
     lent = half * rows
-    sizes = (blocks, dp_count, pipe_count, chunks, rows, width, group, taps_count)
+    halved = chunks // 2
+    sizes = (blocks, dp_count, pipe_count, chunks, halved, rows, width, group, taps_count)
     anywhere = pl.BlockSpec(memory_space=pltpu.HBM)
     vmem = pl.BlockSpec(memory_space=pltpu.VMEM)
     one_sem = pltpu.SemaphoreType.DMA
@@ -702,15 +722,15 @@
         scratch_shapes=[
             pltpu.VMEM((taps_count, channels // width, width), jnp.float32),
             pltpu.VMEM((filter_count, seq_len), jnp.float32),
-            pltpu.VMEM((chunks, per_chunk, lent), jnp.float32),
+            pltpu.VMEM((halved, per_chunk, lent), jnp.float32),
             pltpu.VMEM((chunks, 2 * blocks, rows, width), jnp.bfloat16),
-            pltpu.VMEM((chunks, 2 * half, rows, width), jnp.bfloat16),
-            pltpu.VMEM((chunks, 16, width), jnp.bfloat16),
+            pltpu.VMEM((halved, 2 * half, rows, width), jnp.bfloat16),
+            pltpu.VMEM((halved, 16, width), jnp.bfloat16),
             pltpu.VMEM((chunks, blocks, rows, width), jnp.bfloat16),
-            pltpu.VMEM((chunks, half, rows, width), jnp.bfloat16),
+            pltpu.VMEM((halved, half, rows, width), jnp.bfloat16),
             pltpu.VMEM((dp_count, chunks, per_chunk, seq_len + width), jnp.float32),
-            pltpu.VMEM((chunks, per_chunk, lent + 2 * width), jnp.float32),
-            pltpu.VMEM((chunks, per_chunk, lent + 2 * width), jnp.float32),
+            pltpu.VMEM((halved, per_chunk, lent + 2 * width), jnp.float32),
+            pltpu.VMEM((halved, per_chunk, lent + 2 * width), jnp.float32),
             pltpu.VMEM((seq_len + 8, width), jnp.float32),
             pltpu.VMEM((2, width, seq_len), jnp.bfloat16),
             pltpu.VMEM((width, 2 * seq_len), jnp.bfloat16),
@@ -754,7 +774,7 @@
         rows == 128
         and blocks == 4
         and mesh.shape["pipe"] == 2
-        and own_width % rows == 0
+        and own_width % (2 * rows) == 0
         and rows % group == 0
         and rows // group == 8
         and short_taps.shape[1] <= 8

time: 77.2 us -> 77.1 us (level)
  no operation moved by 1% of the time
where the time goes in v5:
time: 77.1 us; the launch traced here: 76.9 us
  Pallas kernels  71.9 us (93%)
  local copies, waits for them, and re-layouts  4.38 us (6%)
    pallas_call x1, Pallas kernels, fused_body(): pl.pallas_call(functools.partial(fused_kernel, sizes), out_shape=(jax.Sha...  71.9 us
    unnamed x5, local copies, waits for them, and re-layouts  4.38 us

profile of v5, /device:TPU:0, one launch (start us, length us, event | category | flops | bytes accessed | tf_op | source)
XLA Modules:
  0.0 76.9 jit_solution(3788774153079253354)
XLA Ops:
  0.6 71.9 %shard_map.67 = (bf16[128,4096]{1,0:T(8,128)(2,1)}, f32[64,512]{1,0:T(8,128)}, f32[7,1024]{1,0:T(8,128)}) custom-call(bf16[128,4096]{1,0:T(8,128)(2,1)} %bitcast.6, bf16[128,4096]{1,0:T(8,128)(2,1)} %bitcast.7, f32[7,32,128]{2,1,0:T(8,128)} %bitcast.10, f32[1,64,512]{2,1,0:T(8,128)} %filters_all.1), custom_call_target="tpu_custom_call" | custom-call | tf_op jit(solution)/shard_map/pallas_call | solution.py:713
  72.5 1.4 %copy.7 = f32[1,7,1024]{2,0,1:T(1,128)} copy(f32[1,7,1024]{2,1,0:T(8,128)} %bitcast.11) | data formatting | bytes 57344
  73.9 0.0 copy-start
  73.9 2.3 %copy.10 = bf16[1,1,128,4096]{3,2,1,0:T(8,128)(2,1)} copy(bf16[1,1,128,4096]{3,2,1,0:T(8,128)(2,1)} %bitcast.8) | data formatting | bytes 2097152
  76.3 0.0 copy-done
  76.3 0.7 copy.11
Async XLA Ops:
  73.9 2.3 %copy-start = (f32[64,512]{1,0:T(8,128)S(1)}, f32[64,512]{1,0:T(8,128)}, u32[]{:S(2)}) copy-start(f32[64,512]{1,0:T(8,128)} %get-tuple-element.7) | copy-start | bytes 393220

commit v6 on v5

--- a/solution.py
+++ b/solution.py
@@ -478,11 +478,11 @@
                 diagonals[pl.ds(place, 8), :] = folded[0]
 
         def do_filters(index, inner):
-            one_filter(2 * index)
-            one_filter(2 * index + 1)
+            for place in range(4):
+                one_filter(4 * index + place)
             return inner
 
-        lax.fori_loop(0, per_chunk // 2, do_filters, 0)
+        lax.fori_loop(0, per_chunk // 4, do_filters, 0)
         for block in range(feat_blocks):
             here = slice(block * rows, (block + 1) * rows)
             conv_grad[here, :] = conv_cols[:, here].T
@@ -664,7 +664,7 @@
         filter_out[chunk * per_chunk : (chunk + 1) * per_chunk, :] = (
             total[:, :seq_len] * filter_scale
         )
-        tap_out[:, chunk * width : (chunk + 1) * width] = total[:taps_count, seq_len:] * tap_scale
+        tap_out[:, chunk, :] = total[:taps_count, seq_len:] * tap_scale
     drain(shares.at[0 : dp_count - 1], send_share)
 
     @pl.when(is_early)
@@ -715,7 +715,7 @@
         out_shape=(
             jax.ShapeDtypeStruct((rows, channels), jnp.bfloat16),
             jax.ShapeDtypeStruct((filter_count, seq_len), jnp.float32),
-            jax.ShapeDtypeStruct((taps_count, own_width), jnp.float32),
+            jax.ShapeDtypeStruct((taps_count, chunks, width), jnp.float32),
         ),
         in_specs=[anywhere] * 4,
         out_specs=(anywhere, vmem, vmem),
@@ -762,7 +762,11 @@
         short_taps.reshape(taps_count, channels // width, width),
         filters,
     )
-    return (feature_grads[None, None], filter_grads[None], tap_grads[None])
+    return (
+        feature_grads[None, None],
+        filter_grads[None],
+        tap_grads.reshape(1, taps_count, own_width),
+    )
 
 
 def fits_fused(mesh, features, short_taps, filters):

time: 77.1 us -> 75.1 us (0.974)
  Pallas kernels: 71.9 us -> 70.6 us
    pallas_call x1, Pallas kernels: 71.9 us -> 70.6 us  [fused_body(): pl.pallas_call(functools.partial(fused_kernel, sizes), out_shape=(jax.Sha...]
    unnamed x5 -> x7, local copies, waits for them, and re-layouts: 4.38 us -> 3.68 us
where the time goes in v6:
time: 75.1 us; the launch traced here: 74.9 us
  Pallas kernels  70.6 us (94%)
  local copies, waits for them, and re-layouts  3.68 us (5%)
    pallas_call x1, Pallas kernels, fused_body(): pl.pallas_call(functools.partial(fused_kernel, sizes), out_shape=(jax.Sha...  70.6 us
    unnamed x7, local copies, waits for them, and re-layouts  3.68 us

profile of v6, /device:TPU:0, one launch (start us, length us, event | category | flops | bytes accessed | tf_op | source)
XLA Modules:
  0.0 74.9 jit_solution(16569194252417753864)
XLA Ops:
  0.6 70.6 %shard_map.67 = (bf16[128,4096]{1,0:T(8,128)(2,1)}, f32[64,512]{1,0:T(8,128)}, f32[7,8,128]{2,1,0:T(8,128)}) custom-call(bf16[128,4096]{1,0:T(8,128)(2,1)} %bitcast.6, bf16[128,4096]{1,0:T(8,128)(2,1)} %bitcast.7, f32[7,32,128]{2,1,0:T(8,128)} %bitcast.10, f32[1,64,512]{2,1,0:T(8,128)} %filters_all.1), custom_call_target="tpu_custom_call" | custom-call | tf_op jit(solution)/shard_map/pallas_call | solution.py:713
  71.2 0.0 copy-start
  71.2 2.3 %copy.12 = bf16[1,1,128,4096]{3,2,1,0:T(8,128)(2,1)} copy(bf16[1,1,128,4096]{3,2,1,0:T(8,128)(2,1)} %bitcast.8) | data formatting | bytes 2097152
  73.5 0.0 copy-done
  73.5 0.0 copy-start.1
  73.5 0.7 copy.13
  74.2 0.1 copy-done.1
  74.3 0.6 copy.14
Async XLA Ops:
  71.2 2.3 %copy-start = (f32[64,512]{1,0:T(8,128)S(1)}, f32[64,512]{1,0:T(8,128)}, u32[]{:S(2)}) copy-start(f32[64,512]{1,0:T(8,128)} %get-tuple-element.7) | copy-start | bytes 393220
  73.5 0.7 copy-start.1
